TPU v7x, 32 devices: a whole 2x2x4 slice. The times are simulated.
32 devices in a mesh: dp: 8 (over z, y), chan: 4 (over x, core).
Axes of the slice: x: 2, y: 2, z: 4, core: 2. Of those that a mesh axis runs over, the one named last changes fastest.
Arguments:
- noisy: bfloat16 [16, 32, 32, 512], P('dp', None, None, 'chan'), may hold values from -6 to 6
- noise: float32 [16, 32, 32, 512], P('dp', None, None, 'chan'), may hold values from -6 to 6
- timesteps: int32 [16], P('dp'), may hold values from 0 to 999
- classes: int32 [16], P('dp'), may hold values from 0 to 999
- sample_weight: float32 [16], P('dp'), may hold values from 0.5 to 7.5
- conv_in: float32 [3, 4608, 512], P(None, 'dp', 'chan'), may hold values from -0.09375 to 0.09375
- conv_out: float32 [2, 4608, 512], P(None, 'dp', 'chan'), may hold values from -0.09375 to 0.09375
- emb_proj: float32 [2, 1024, 1024], P(None, 'dp', 'chan'), may hold values from -0.09375 to 0.09375
- attn_weight: float32 [512, 2048], P('dp', 'chan'), may hold values from -1.41421356 to 1.41421356
- time_in: float32 [256, 1024], P('dp', 'chan'), may hold values from -0.375 to 0.375
- emb_out: float32 [1024, 2024], P('dp', 'chan'), may hold values from -4 to 4
- norms: float32 [6, 2, 512], P(None, None, 'chan'), may hold values from -0.4 to 1.75
- conv_in_rows: float32 [3, 4608], P(None, 'dp'), may hold values from 9.313226e-11 to 1.3969839e-09
- conv_in_cols: float32 [3, 512], P(None, 'chan'), may hold values from 9.313226e-11 to 1.3969839e-09
- conv_out_rows: float32 [2, 4608], P(None, 'dp'), may hold values from 9.313226e-11 to 1.3969839e-09
- conv_out_cols: float32 [2, 512], P(None, 'chan'), may hold values from 9.313226e-11 to 1.3969839e-09
- emb_proj_rows: float32 [2, 1024], P(None, 'dp'), may hold values from 9.313226e-11 to 1.3969839e-09
- emb_proj_cols: float32 [2, 1024], P(None, 'chan'), may hold values from 9.313226e-11 to 1.3969839e-09
- attn_rows: float32 [512], P('dp'), may hold values from 5.820766e-08 to 2.3283064e-07
- attn_cols: float32 [2048], P('chan'), may hold values from 9.313226e-11 to 1.3969839e-09
- time_rows: float32 [256], P('dp'), may hold values from 9.313226e-11 to 1.3969839e-09
- time_cols: float32 [1024], P('chan'), may hold values from 9.313226e-11 to 1.3969839e-09
- embout_rows: float32 [1024], P('dp'), may hold values from 9.313226e-11 to 1.3969839e-09
- embout_cols: float32 [2024], P('chan'), may hold values from 9.313226e-11 to 1.3969839e-09
- norm_second: float32 [6, 2, 512], P(None, None, 'chan'), may hold values from 9.536743e-07 to 3.8146973e-06
Outputs:
- loss: float32 [], replicated
- conv_in_grad: float32 [3, 4608, 512], P(None, 'dp', 'chan')
- conv_in_rows_new: float32 [3, 4608], P(None, 'dp')
- conv_in_cols_new: float32 [3, 512], P(None, 'chan')
- conv_in_new: float32 [3, 4608, 512], P(None, 'dp', 'chan')
- conv_out_grad: float32 [2, 4608, 512], P(None, 'dp', 'chan')
- conv_out_rows_new: float32 [2, 4608], P(None, 'dp')
- conv_out_cols_new: float32 [2, 512], P(None, 'chan')
- conv_out_new: float32 [2, 4608, 512], P(None, 'dp', 'chan')
- emb_proj_grad: float32 [2, 1024, 1024], P(None, 'dp', 'chan')
- emb_proj_rows_new: float32 [2, 1024], P(None, 'dp')
- emb_proj_cols_new: float32 [2, 1024], P(None, 'chan')
- emb_proj_new: float32 [2, 1024, 1024], P(None, 'dp', 'chan')
- attn_grad: float32 [512, 2048], P('dp', 'chan')
- attn_rows_new: float32 [512], P('dp')
- attn_cols_new: float32 [2048], P('chan')
- attn_new: float32 [512, 2048], P('dp', 'chan')
- time_grad: float32 [256, 1024], P('dp', 'chan')
- time_rows_new: float32 [256], P('dp')
- time_cols_new: float32 [1024], P('chan')
- time_new: float32 [256, 1024], P('dp', 'chan')
- embout_grad: float32 [1024, 2024], P('dp', 'chan')
- embout_rows_new: float32 [1024], P('dp')
- embout_cols_new: float32 [2024], P('chan')
- embout_new: float32 [1024, 2024], P('dp', 'chan')
- norm_grad: float32 [6, 2, 512], P(None, None, 'chan')
- norm_second_new: float32 [6, 2, 512], P(None, None, 'chan')
- norms_new: float32 [6, 2, 512], P(None, None, 'chan')
All inputs are finite; a program needn't handle non-finite values.
Results may differ from a plain program's by a relative error of at most 0.02.
Values may be sent and summed in bfloat16 or wider, within the bound.
A program may use at most 192 MiB of HBM per device.

v0:
```python
import math

import jax
import jax.numpy as jnp
from jax import lax
from jax.sharding import PartitionSpec as P

C = 512
HEADS = 8
GROUPS = 32
TF = 256
STEP = 10
QB = 512


single = jnp.float32
narrow = jnp.bfloat16
step_rate = 0.5
floor_scale = 0.001
tiny_square = 1e-30
norm_eps = 1e-05


def shifted_view(values, shift_y, shift_x):
    padded = jnp.pad(values, ((0, 0), (1, 1), (1, 1), (0, 0)))
    height, across = (values.shape[1], values.shape[2])
    return padded[:, 1 + shift_y : 1 + shift_y + height, 1 + shift_x : 1 + shift_x + across, :]


def tap_offsets():
    return [(tap_index // 3 - 1, tap_index % 3 - 1) for tap_index in range(9)]


def spread(local_act):
    return lax.all_gather(local_act, "chan", axis=3, tiled=True)


def spread_back(partial_sum):
    return lax.psum_scatter(
        partial_sum.astype(jnp.bfloat16), "chan", scatter_dimension=3, tiled=True
    ).astype(jnp.float32)


def collect(partial_sum):
    return lax.psum_scatter(
        partial_sum.astype(jnp.bfloat16), "chan", scatter_dimension=3, tiled=True
    ).astype(jnp.float32)


def collect_back(grad_local):
    return lax.all_gather(grad_local, "chan", axis=3, tiled=True)


def conv_gathered(full_in, kernel):
    channels = full_in.shape[3]
    summed = 0.0
    for tap_index, (shift_y, shift_x) in enumerate(tap_offsets()):
        kernel_tap = kernel[tap_index * channels : (tap_index + 1) * channels]
        summed = summed + jnp.einsum(
            "bhwi,io->bhwo",
            shifted_view(full_in, shift_y, shift_x),
            kernel_tap,
            preferred_element_type=single,
        )
    return summed


def conv_gathered_back(full_in, kernel, grad_out):
    channels = full_in.shape[3]
    pieces = []
    partial_sum = 0.0
    for tap_index, (shift_y, shift_x) in enumerate(tap_offsets()):
        kernel_tap = kernel[tap_index * channels : (tap_index + 1) * channels]
        pieces.append(
            jnp.einsum(
                "bhwi,bhwo->io",
                shifted_view(full_in, shift_y, shift_x),
                grad_out,
                preferred_element_type=single,
            )
        )
        returned = jnp.einsum("bhwo,io->bhwi", grad_out, kernel_tap, preferred_element_type=single)
        partial_sum = partial_sum + shifted_view(returned, -shift_y, -shift_x)
    return (jnp.concatenate(pieces, 0), partial_sum)


def conv_split(local_in, kernel):
    channels = kernel.shape[0] // 9
    summed = 0.0
    for tap_index, (shift_y, shift_x) in enumerate(tap_offsets()):
        kernel_tap = kernel[tap_index * channels : (tap_index + 1) * channels]
        product = jnp.einsum("bhwi,oi->bhwo", local_in, kernel_tap, preferred_element_type=single)
        summed = summed + shifted_view(product, shift_y, shift_x)
    return summed


def conv_split_back(local_in, kernel, full_grad):
    channels = kernel.shape[0] // 9
    pieces = []
    grad_in = 0.0
    for tap_index, (shift_y, shift_x) in enumerate(tap_offsets()):
        kernel_tap = kernel[tap_index * channels : (tap_index + 1) * channels]
        moved = shifted_view(full_grad, -shift_y, -shift_x)
        pieces.append(jnp.einsum("bhwo,bhwi->oi", moved, local_in, preferred_element_type=single))
        grad_in = grad_in + jnp.einsum(
            "bhwo,oi->bhwi", moved, kernel_tap, preferred_element_type=single
        )
    return (jnp.concatenate(pieces, 0), grad_in)


def group_norm(values, gain_vec, bias_vec):
    group_size = C // GROUPS
    images, height, across, channels = values.shape
    grouped = values.reshape(images, height * across, channels // group_size, group_size)
    center = grouped - jnp.mean(grouped, (1, 3), keepdims=True)
    variance = jnp.mean(center * center, (1, 3), keepdims=True)
    return (center * lax.rsqrt(variance + norm_eps)).reshape(values.shape) * gain_vec + bias_vec


def plain_norm(values, norm_params):
    return group_norm(values, norm_params[0], norm_params[1])


def act_norm(values, norm_params):
    return jax.nn.silu(group_norm(values, norm_params[0], norm_params[1]))


def mid_block(inner_act, norm_params, modulate):
    images, channels = (modulate.shape[0], inner_act.shape[3])
    paired = modulate.reshape(images, channels, 2)
    mixed = (
        group_norm(inner_act, norm_params[0], norm_params[1]) * (1.0 + paired[:, None, None, :, 0])
        + paired[:, None, None, :, 1]
    )
    return jax.nn.silu(mixed)


def res_forward(stream, kernel_in, kernel_out, modulator, norm_pair, context):
    entry_full = spread(act_norm(stream, norm_pair[0]).astype(narrow))
    inner_act = conv_gathered(entry_full, kernel_in)
    modulate = jnp.dot(context, modulator, preferred_element_type=single)
    hidden = mid_block(inner_act, norm_pair[1], modulate).astype(narrow)
    branch = collect(conv_split(hidden, kernel_out))
    return (stream + branch, (entry_full, inner_act, modulate, hidden))


def res_backward(stream, kernel_in, kernel_out, modulator, norm_pair, context, saved, grad_out):
    entry_full, inner_act, modulate, hidden = saved
    branch_grad = collect_back(grad_out.astype(narrow))
    out_kernel_grad, hidden_grad = conv_split_back(hidden, kernel_out, branch_grad)
    _, pullback = jax.vjp(mid_block, inner_act, norm_pair[1], modulate)
    inner_grad, second_norm_grad, modulate_grad = pullback(hidden_grad)
    modulate_low = modulate_grad.astype(narrow)
    modulator_grad = jnp.einsum("be,bj->ej", context, modulate_low, preferred_element_type=single)
    context_part = jnp.einsum("bj,ej->be", modulate_low, modulator, preferred_element_type=single)
    in_kernel_grad, partial_sum = conv_gathered_back(
        entry_full, kernel_in, inner_grad.astype(narrow)
    )
    entry_grad = spread_back(partial_sum)
    _, pullback = jax.vjp(act_norm, stream, norm_pair[0])
    stream_grad, first_norm_grad = pullback(entry_grad)
    grads = (
        in_kernel_grad,
        out_kernel_grad,
        modulator_grad,
        jnp.stack([first_norm_grad, second_norm_grad]),
    )
    return (grad_out + stream_grad, grads, context_part)


def attend_forward(queries, keys_low, values_low):
    images, pixels, heads_here, head_size = queries.shape
    scale_factor = head_size ** (-0.5)
    stacked = jnp.moveaxis(queries.reshape(images, pixels // QB, QB, heads_here, head_size), 1, 0)

    def score_block(query_block):
        scores = (
            jnp.einsum("bqhd,bkhd->bhqk", query_block, keys_low, preferred_element_type=single)
            * scale_factor
        )
        row_max = jnp.max(scores, -1, keepdims=True)
        exponent = jnp.exp(scores - row_max)
        row_total = jnp.sum(exponent, -1, keepdims=True)
        weights = (exponent / row_total).astype(narrow)
        attended = jnp.einsum("bhqk,bkhd->bqhd", weights, values_low, preferred_element_type=single)
        return (attended, (row_max + jnp.log(row_total))[..., 0])

    attended, log_total = lax.map(score_block, stacked)
    return (jnp.moveaxis(attended, 0, 1).reshape(images, pixels, heads_here, head_size), log_total)


def attend_backward(queries, keys_low, values_low, log_total, grad_attended):
    images, pixels, heads_here, head_size = queries.shape
    scale_factor = head_size ** (-0.5)
    stacked = jnp.moveaxis(queries.reshape(images, pixels // QB, QB, heads_here, head_size), 1, 0)
    stacked_grad = jnp.moveaxis(
        grad_attended.reshape(images, pixels // QB, QB, heads_here, head_size), 1, 0
    )

    def score_step(carried, items):
        keys_grad, values_grad = carried
        query_block, log_block, grad_block = items
        scores = (
            jnp.einsum("bqhd,bkhd->bhqk", query_block, keys_low, preferred_element_type=single)
            * scale_factor
        )
        weights = jnp.exp(scores - log_block[..., None])
        values_grad = values_grad + jnp.einsum(
            "bhqk,bqhd->bkhd", weights.astype(narrow), grad_block, preferred_element_type=single
        )
        weight_grad = jnp.einsum(
            "bqhd,bkhd->bhqk", grad_block, values_low, preferred_element_type=single
        )
        score_grad = weights * (weight_grad - jnp.sum(weights * weight_grad, -1, keepdims=True))
        score_low = (score_grad * scale_factor).astype(narrow)
        query_grad = jnp.einsum(
            "bhqk,bkhd->bqhd", score_low, keys_low, preferred_element_type=single
        )
        keys_grad = keys_grad + jnp.einsum(
            "bhqk,bqhd->bkhd", score_low, query_block, preferred_element_type=single
        )
        return ((keys_grad, values_grad), query_grad)

    zeroed = jnp.zeros(keys_low.shape, single)
    (keys_grad, values_grad), query_grad = lax.scan(
        score_step, (zeroed, zeroed), (stacked, log_total, stacked_grad)
    )
    query_grad = jnp.moveaxis(query_grad, 0, 1).reshape(queries.shape)
    return (query_grad, keys_grad, values_grad)


def attn_forward(stream, kernel, norm_one):
    images, height, across, local_ch = stream.shape
    pixels = height * across
    heads_here = local_ch * HEADS // C
    head_size = C // HEADS
    entry_full = spread(plain_norm(stream, norm_one).astype(narrow)).reshape(images, pixels, -1)
    qkv_low = jnp.einsum(
        "bpc,cj->bpj", entry_full, kernel[:, : 3 * local_ch], preferred_element_type=single
    ).astype(narrow)
    qkv_low = qkv_low.reshape(images, pixels, heads_here, 3, head_size)
    attended, log_total = attend_forward(
        qkv_low[:, :, :, 0], qkv_low[:, :, :, 1], qkv_low[:, :, :, 2]
    )
    attended_low = attended.reshape(images, pixels, local_ch).astype(narrow)
    partial_sum = jnp.einsum(
        "bpi,oi->bpo", attended_low, kernel[:, 3 * local_ch :], preferred_element_type=single
    )
    branch = collect(partial_sum.reshape(images, height, across, -1))
    return (stream + branch, (entry_full, qkv_low, log_total, attended_low))


def attn_backward(stream, kernel, norm_one, saved, grad_out):
    entry_full, qkv_low, log_total, attended_low = saved
    images, height, across, local_ch = stream.shape
    pixels = height * across
    branch_grad = collect_back(grad_out.astype(narrow)).reshape(images, pixels, -1)
    proj_grad = jnp.einsum("bpo,bpi->oi", branch_grad, attended_low, preferred_element_type=single)
    attended_grad = jnp.einsum(
        "bpo,oi->bpi", branch_grad, kernel[:, 3 * local_ch :], preferred_element_type=single
    ).astype(narrow)
    query_grad, keys_grad, values_grad = attend_backward(
        qkv_low[:, :, :, 0],
        qkv_low[:, :, :, 1],
        qkv_low[:, :, :, 2],
        log_total,
        attended_grad.reshape(qkv_low[:, :, :, 0].shape),
    )
    qkv_grad = (
        jnp.stack([query_grad, keys_grad, values_grad], 3)
        .reshape(images, pixels, 3 * local_ch)
        .astype(narrow)
    )
    qkv_kernel_grad = jnp.einsum("bpc,bpj->cj", entry_full, qkv_grad, preferred_element_type=single)
    partial_sum = jnp.einsum(
        "bpj,cj->bpc", qkv_grad, kernel[:, : 3 * local_ch], preferred_element_type=single
    )
    entry_grad = spread_back(partial_sum.reshape(images, height, across, -1))
    _, pullback = jax.vjp(plain_norm, stream, norm_one)
    stream_grad, norm_grad = pullback(entry_grad)
    return (grad_out + stream_grad, jnp.concatenate([qkv_kernel_grad, proj_grad], 1), norm_grad)


def pixel_total(stream):
    return float(stream.shape[0] * lax.axis_size("dp") * stream.shape[1] * stream.shape[2] * C)


def head_forward(stream, kernel, norm_one, noise, sample_weight):
    entry_full = spread(act_norm(stream, norm_one).astype(narrow))
    predicted = conv_gathered(entry_full, kernel)
    residual_error = predicted - noise
    loss_part = jnp.sum(
        sample_weight[:, None, None, None] * residual_error * residual_error
    ) / pixel_total(stream)
    return (loss_part, (entry_full, residual_error))


def head_backward(stream, kernel, norm_one, sample_weight, saved):
    entry_full, residual_error = saved
    predict_grad = (
        2.0 * sample_weight[:, None, None, None] * residual_error / pixel_total(stream)
    ).astype(narrow)
    kernel_grad, partial_sum = conv_gathered_back(entry_full, kernel, predict_grad)
    entry_grad = spread_back(partial_sum)
    _, pullback = jax.vjp(act_norm, stream, norm_one)
    stream_grad, norm_grad = pullback(entry_grad)
    return (stream_grad, kernel_grad, norm_grad)


def embed_forward(timesteps, classes, time_kernel, out_kernel):
    half_count = TF // 2
    frequency = jnp.exp(-math.log(10000.0) * jnp.arange(half_count, dtype=single) / half_count)
    angles = timesteps.astype(single)[:, None] * frequency[None, :]
    sinusoid = jnp.concatenate([jnp.cos(angles), jnp.sin(angles)], 1).astype(narrow)
    time_pre = jnp.dot(sinusoid, time_kernel, preferred_element_type=single)
    hidden = jax.nn.silu(time_pre).astype(narrow)
    class_here = out_kernel.shape[1] - hidden.shape[1]
    first_class = lax.axis_index("chan") * class_here
    onehot = (classes[:, None] == first_class + jnp.arange(class_here)[None, :]).astype(narrow)
    joined = jnp.concatenate([hidden, onehot], 1)
    partial_sum = jnp.einsum("bj,ej->be", joined, out_kernel, preferred_element_type=single)
    embedding = lax.psum(partial_sum, "chan")
    return (embedding, (sinusoid, time_pre, joined))


def embed_backward(embedding, saved, out_kernel, context_grad):
    sinusoid, time_pre, joined = saved
    _, pullback = jax.vjp(jax.nn.silu, embedding)
    (embed_grad,) = pullback(context_grad)
    embed_low = embed_grad.astype(narrow)
    embout_grad = jnp.einsum("be,bj->ej", embed_low, joined, preferred_element_type=single)
    joined_grad = jnp.einsum("be,ej->bj", embed_low, out_kernel, preferred_element_type=single)
    _, pullback = jax.vjp(jax.nn.silu, time_pre)
    (pre_grad,) = pullback(joined_grad[:, : time_pre.shape[1]])
    time_grad = jnp.einsum(
        "bt,be->te", sinusoid, pre_grad.astype(narrow), preferred_element_type=single
    )
    return (time_grad, embout_grad)


def pack_flat(members):
    return jnp.concatenate([member.reshape(-1) for member in members])


def unpack_flat(vector, shape_list):
    pieces = []
    offset = 0
    for array_shape in shape_list:
        extent = math.prod(array_shape)
        pieces.append(vector[offset : offset + extent].reshape(array_shape))
        offset += extent
    return pieces


def per_device(
    noisy,
    noise,
    timesteps,
    classes,
    sample_weight,
    conv_in,
    conv_out,
    emb_proj,
    attn_weight,
    time_in,
    emb_out,
    norms,
    conv_in_rows,
    conv_in_cols,
    conv_out_rows,
    conv_out_cols,
    emb_proj_rows,
    emb_proj_cols,
    attn_rows,
    attn_cols,
    time_rows,
    time_cols,
    embout_rows,
    embout_cols,
    norm_second,
):
    masters = [conv_in, conv_out, emb_proj, attn_weight[None], time_in[None], emb_out[None]]
    lowered = [master.astype(narrow) for master in masters]
    gathered = (
        lax.all_gather(lowered[0], "dp", axis=1, tiled=True),
        lax.all_gather(lowered[1], "dp", axis=1, tiled=True),
        lax.all_gather(lowered[2], "dp", axis=1, tiled=True),
        lax.all_gather(lowered[3], "dp", axis=1, tiled=True),
        lax.all_gather(lowered[4], "dp", axis=1, tiled=True),
        lax.all_gather(lowered[5], "dp", axis=1, tiled=True),
    )
    kernels_in, kernels_out, modulators, attn_full, time_full, embout_full = gathered
    stream0 = noisy.astype(single)
    embedding, embed_saved = embed_forward(timesteps, classes, time_full[0], embout_full[0])
    context = jax.nn.silu(embedding).astype(narrow)
    stream1, saved_first = res_forward(
        stream0, kernels_in[0], kernels_out[0], modulators[0], norms[0:2], context
    )
    stream2, saved_attn = attn_forward(stream1, attn_full[0], norms[2])
    stream3, saved_second = res_forward(
        stream2, kernels_in[1], kernels_out[1], modulators[1], norms[3:5], context
    )
    loss_part, head_saved = head_forward(stream3, kernels_in[2], norms[5], noise, sample_weight)
    again = (
        lax.all_gather(lowered[0], "dp", axis=1, tiled=True),
        lax.all_gather(lowered[1], "dp", axis=1, tiled=True),
        lax.all_gather(lowered[2], "dp", axis=1, tiled=True),
        lax.all_gather(lowered[3], "dp", axis=1, tiled=True),
        lax.all_gather(lowered[4], "dp", axis=1, tiled=True),
        lax.all_gather(lowered[5], "dp", axis=1, tiled=True),
    )
    kernels_in, kernels_out, modulators, attn_full, time_full, embout_full = again
    _, head_saved = head_forward(stream3, kernels_in[2], norms[5], noise, sample_weight)
    grad3, head_kernel_grad, head_norm_grad = head_backward(
        stream3, kernels_in[2], norms[5], sample_weight, head_saved
    )
    _, saved_second = res_forward(
        stream2, kernels_in[1], kernels_out[1], modulators[1], norms[3:5], context
    )
    grad2, second_grads, context_second = res_backward(
        stream2,
        kernels_in[1],
        kernels_out[1],
        modulators[1],
        norms[3:5],
        context,
        saved_second,
        grad3,
    )
    _, saved_attn = attn_forward(stream1, attn_full[0], norms[2])
    grad1, attn_kernel_grad, attn_norm_grad = attn_backward(
        stream1, attn_full[0], norms[2], saved_attn, grad2
    )
    _, saved_first = res_forward(
        stream0, kernels_in[0], kernels_out[0], modulators[0], norms[0:2], context
    )
    grad0, first_grads, context_first = res_backward(
        stream0,
        kernels_in[0],
        kernels_out[0],
        modulators[0],
        norms[0:2],
        context,
        saved_first,
        grad1,
    )
    context_grad = lax.psum(context_first + context_second, "chan")
    time_grad, embout_grad = embed_backward(embedding, embed_saved, embout_full[0], context_grad)
    local_grads = [
        jnp.stack([first_grads[0], second_grads[0], head_kernel_grad]),
        jnp.stack([first_grads[1], second_grads[1]]),
        jnp.stack([first_grads[2], second_grads[2]]),
        attn_kernel_grad[None],
        time_grad[None],
        embout_grad[None],
    ]
    norm_local = jnp.concatenate(
        [first_grads[3], attn_norm_grad[None], second_grads[3], head_norm_grad[None]], 0
    )
    reduced = (
        lax.psum_scatter(local_grads[0], "dp", scatter_dimension=1, tiled=True),
        lax.psum_scatter(local_grads[1], "dp", scatter_dimension=1, tiled=True),
        lax.psum_scatter(local_grads[2], "dp", scatter_dimension=1, tiled=True),
        lax.psum_scatter(local_grads[3], "dp", scatter_dimension=1, tiled=True),
        lax.psum_scatter(local_grads[4], "dp", scatter_dimension=1, tiled=True),
        lax.psum_scatter(local_grads[5], "dp", scatter_dimension=1, tiled=True),
    )
    decay_rate = 1.0 - STEP ** (-0.8)
    dp_count = lax.axis_size("dp")
    chan_count = lax.axis_size("chan")
    rows_old = [
        conv_in_rows,
        conv_out_rows,
        emb_proj_rows,
        attn_rows[None],
        time_rows[None],
        embout_rows[None],
    ]
    cols_old = [
        conv_in_cols,
        conv_out_cols,
        emb_proj_cols,
        attn_cols[None],
        time_cols[None],
        embout_cols[None],
    ]
    squares = [gradient * gradient + tiny_square for gradient in reduced]
    full_rows = [squared.shape[1] * dp_count for squared in squares]
    full_cols = [squared.shape[2] * chan_count for squared in squares]
    row_parts = [jnp.sum(squared, 2) for squared in squares]
    col_parts = [jnp.sum(squared, 1) for squared in squares]
    row_shapes = [member.shape for member in row_parts]
    col_shapes = [member.shape for member in col_parts]
    norm_width = norm_local.shape[2]
    row_totals = unpack_flat(lax.psum(pack_flat(row_parts), "chan"), row_shapes)
    rows_new = [
        decay_rate * rows_old[position]
        + (1.0 - decay_rate) * row_totals[position] / full_cols[position]
        for position in range(6)
    ]
    row_sums_local = [jnp.sum(member, 1) for member in rows_new]
    col_vector, norm_total = lax.psum((pack_flat(col_parts + row_sums_local), norm_local), "dp")
    col_pieces = unpack_flat(col_vector, col_shapes + [(member.shape[0],) for member in rows_new])
    col_totals = col_pieces[:6]
    row_means = [col_pieces[6 + position] / full_rows[position] for position in range(6)]
    cols_new = [
        decay_rate * cols_old[position]
        + (1.0 - decay_rate) * col_totals[position] / full_rows[position]
        for position in range(6)
    ]
    updates = [
        reduced[position]
        * lax.rsqrt(rows_new[position] / row_means[position][:, None])[:, :, None]
        * lax.rsqrt(cols_new[position])[:, None, :]
        for position in range(6)
    ]
    second_new = decay_rate * norm_second + (1.0 - decay_rate) * (
        norm_total * norm_total + tiny_square
    )
    norm_update = norm_total * lax.rsqrt(second_new)
    update_squares = pack_flat([jnp.sum(member * member, (1, 2)) for member in updates])
    weight_squares = pack_flat([jnp.sum(master * master, (1, 2)) for master in masters])
    norm_update_sq = jnp.sum(norm_update * norm_update, 2) / dp_count
    norm_weight_sq = jnp.sum(norms * norms, 2) / dp_count
    update_total, weight_total, norm_update_total, norm_weight_total, loss = lax.psum(
        (update_squares, weight_squares, norm_update_sq, norm_weight_sq, loss_part), ("dp", "chan")
    )
    layer_shapes = [(member.shape[0],) for member in masters]
    update_sums = unpack_flat(update_total, layer_shapes)
    weight_sums = unpack_flat(weight_total, layer_shapes)
    results = [loss]
    for position in range(6):
        entries = float(full_rows[position] * full_cols[position])
        clip_factor = jnp.maximum(1.0, jnp.sqrt(update_sums[position] / entries))
        scale_factor = jnp.maximum(floor_scale, jnp.sqrt(weight_sums[position] / entries))
        weight_new = (
            masters[position]
            - (step_rate * scale_factor / clip_factor)[:, None, None] * updates[position]
        )
        if position >= 3:
            results += [
                reduced[position][0],
                rows_new[position][0],
                cols_new[position][0],
                weight_new[0],
            ]
        else:
            results += [reduced[position], rows_new[position], cols_new[position], weight_new]
    norm_entries = float(norm_width * chan_count)
    norm_clip = jnp.maximum(1.0, jnp.sqrt(norm_update_total / norm_entries))
    norm_scale = jnp.maximum(floor_scale, jnp.sqrt(norm_weight_total / norm_entries))
    norms_new = norms - (step_rate * norm_scale / norm_clip)[:, :, None] * norm_update
    results += [norm_total, second_new, norms_new]
    return (
        results[0],
        results[1],
        results[2],
        results[3],
        results[4],
        results[5],
        results[6],
        results[7],
        results[8],
        results[9],
        results[10],
        results[11],
        results[12],
        results[13],
        results[14],
        results[15],
        results[16],
        results[17],
        results[18],
        results[19],
        results[20],
        results[21],
        results[22],
        results[23],
        results[24],
        results[25],
        results[26],
        results[27],
    )


def solution(mesh):
    in_specs = (
        P("dp", None, None, "chan"),
        P("dp", None, None, "chan"),
        P("dp"),
        P("dp"),
        P("dp"),
        P(None, "dp", "chan"),
        P(None, "dp", "chan"),
        P(None, "dp", "chan"),
        P("dp", "chan"),
        P("dp", "chan"),
        P("dp", "chan"),
        P(None, None, "chan"),
        P(None, "dp"),
        P(None, "chan"),
        P(None, "dp"),
        P(None, "chan"),
        P(None, "dp"),
        P(None, "chan"),
        P("dp"),
        P("chan"),
        P("dp"),
        P("chan"),
        P("dp"),
        P("chan"),
        P(None, None, "chan"),
    )
    out_specs = (
        P(),
        P(None, "dp", "chan"),
        P(None, "dp"),
        P(None, "chan"),
        P(None, "dp", "chan"),
        P(None, "dp", "chan"),
        P(None, "dp"),
        P(None, "chan"),
        P(None, "dp", "chan"),
        P(None, "dp", "chan"),
        P(None, "dp"),
        P(None, "chan"),
        P(None, "dp", "chan"),
        P("dp", "chan"),
        P("dp"),
        P("chan"),
        P("dp", "chan"),
        P("dp", "chan"),
        P("dp"),
        P("chan"),
        P("dp", "chan"),
        P("dp", "chan"),
        P("dp"),
        P("chan"),
        P("dp", "chan"),
        P(None, None, "chan"),
        P(None, None, "chan"),
        P(None, None, "chan"),
    )
    return jax.shard_map(
        per_device, mesh=mesh, in_specs=in_specs, out_specs=out_specs, check_vma=False
    )
```

profile of v0, /device:TPU:12, one launch (start us, length us, event | category | flops | bytes accessed | tf_op | source)
XLA Modules:
  0.0 1806.1 jit_solution(16321763227213785681)
XLA Ops:
  20.2 28.4 %all-gather = bf16[256,256]{1,0:T(8,128)(2,1)S(1)} all-gather(bf16[32,256]{1,0:T(8,128)(2,1)S(1)} %get-tuple-element.477), channel_id=2, replica_groups=mesh['dp'=8,'chan'=4] {'dp'}, dimensions={0}, use_global_device_ids=true | all-gather | bytes 147456 | tf_op jit(solution)/shard_map/all_gather | solution.py:389
  49.4 33.8 %all-gather.1 = bf16[1024,506]{1,0:T(8,128)(2,1)S(1)} all-gather(bf16[128,506]{1,0:T(8,128)(2,1)S(1)} %get-tuple-element.471), channel_id=3, replica_groups=mesh['dp'=8,'chan'=4] {'dp'}, dimensions={0}, use_global_device_ids=true | all-gather | bytes 1165824 | tf_op jit(solution)/shard_map/all_gather | solution.py:390
  84.5 6.3 psum.70
  93.6 49.8 %all-gather.16.cloned.1.call-done = bf16[3,4608,128]{2,1,0:T(8,128)(2,1)} async-done(((bf16[3,576,128]{2,1,0:T(8,128)(2,1)}), bf16[3,4608,128]{2,1,0:T(8,128)(2,1)}) %all-gather.16.cloned.1.call-update) | async-done | bytes 3538960 | tf_op jit(solution)/shard_map/all_gather | solution.py:385
  160.5 36.4 %all-gather.20.cloned.1.call-done = bf16[2,4608,128]{2,1,0:T(8,128)(2,1)} async-done(((bf16[2,576,128]{2,1,0:T(8,128)(2,1)}), bf16[2,4608,128]{2,1,0:T(8,128)(2,1)}) %all-gather.20.cloned.1.call-update) | async-done | bytes 2359312 | tf_op jit(solution)/shard_map/all_gather | solution.py:386
  223.7 10.9 fusion.105
  234.6 12.0 copy.252
  246.6 12.1 reshape.845
  258.7 31.0 %reduce-scatter.37.cloned.1.call-done = bf16[128,2048]{1,0:T(8,128)(2,1)} async-done(((bf16[512,2048]{1,0:T(8,128)(2,1)}), bf16[128,2048]{1,0:T(8,128)(2,1)}) %reduce-scatter.37.cloned.1.call-update) | async-done | bytes 524304
  299.4 29.6 %all-gather.2 = bf16[512,512]{1,0:T(8,128)(2,1)S(1)} all-gather(bf16[64,512]{1,0:T(8,128)(2,1)S(1)} %get-tuple-element.475), channel_id=4, replica_groups=mesh['dp'=8,'chan'=4] {'dp'}, dimensions={0}, use_global_device_ids=true | all-gather | bytes 589824 | tf_op jit(solution)/shard_map/all_gather | solution.py:388
  332.5 19.4 %while.37 = (s32[]{:T(128)}, bf16[2,2,512,2,64]{2,4,3,1,0:T(8,128)(2,1)S(1)}, bf16[2,2,512,2,64]{2,4,3,1,0:T(8,128)(2,1)S(1)}, bf16[2,1024,2,64]{1,3,2,0:T(8,128...) while((s32[]{:T(128)}, bf16[2,2,512,2,64]{2,4,3,1,0:T(8,128)(2,1)S(1)}, ...), condition=%wide.region_17.18_spmd, body=%wide.region_14.17_spmd.sunk | while | flops 547357696 | bytes 18628684 | solution.py:188
  332.5 4.8 fusion.769
  337.3 4.8 fusion.770
  342.2 4.8 fusion.769
  347.0 4.8 fusion.770
  359.4 12.5 copy.254
  371.9 12.1 reshape.847
  384.1 33.6 %reduce-scatter.39.cloned.1.call-done = bf16[128,2048]{1,0:T(8,128)(2,1)} async-done(((bf16[512,2048]{1,0:T(8,128)(2,1)}), bf16[128,2048]{1,0:T(8,128)(2,1)}) %reduce-scatter.39.cloned.1.call-update) | async-done | bytes 524304
  427.9 21.9 %all-gather.24.cloned.1.call-done = bf16[2,32,32,512]{3,2,1,0:T(8,128)(2,1)} async-done(((bf16[2,32,32,128]{3,2,1,0:T(8,128)(2,1)}), bf16[2,32,32,512]{3,2,1,0:T(8,128)(2,1)}) %all-gather.24.cloned.1.call-update) | async-done | bytes 2097168 | tf_op jit(solution)/shard_map/all_gather | solution.py:35
  493.4 12.2 fusion.114
  505.7 12.5 copy.256
  518.2 12.1 reshape.849
  530.4 31.6 %reduce-scatter.41.cloned.1.call-done = bf16[128,2048]{1,0:T(8,128)(2,1)} async-done(((bf16[512,2048]{1,0:T(8,128)(2,1)}), bf16[128,2048]{1,0:T(8,128)(2,1)}) %reduce-scatter.41.cloned.1.call-update) | async-done | bytes 524304
  571.3 22.7 %all-gather.26.cloned.1.call-done = bf16[2,32,32,512]{3,2,1,0:T(8,128)(2,1)} async-done(((bf16[2,32,32,128]{3,2,1,0:T(8,128)(2,1)}), bf16[2,32,32,512]{3,2,1,0:T(8,128)(2,1)}) %all-gather.26.cloned.1.call-update) | async-done | bytes 2097168 | tf_op jit(solution)/shard_map/all_gather | solution.py:35
  623.7 12.6 fusion.123
  636.3 12.5 copy.258
  648.8 12.1 reshape.851
  661.0 31.5 %reduce-scatter.43.cloned.1.call-done = bf16[128,2048]{1,0:T(8,128)(2,1)} async-done(((bf16[512,2048]{1,0:T(8,128)(2,1)}), bf16[128,2048]{1,0:T(8,128)(2,1)}) %reduce-scatter.43.cloned.1.call-update) | async-done | bytes 524304
  705.3 22.8 %all-gather.28.cloned.1.call-done = bf16[2,32,32,512]{3,2,1,0:T(8,128)(2,1)} async-done(((bf16[2,32,32,128]{3,2,1,0:T(8,128)(2,1)}), bf16[2,32,32,512]{3,2,1,0:T(8,128)(2,1)}) %all-gather.28.cloned.1.call-update) | async-done | bytes 2097168 | tf_op jit(solution)/shard_map/all_gather | solution.py:51
  777.0 12.2 fusion.132
  789.3 12.5 copy.260
  801.8 12.1 reshape.853
  814.0 31.5 %reduce-scatter.45.cloned.1.call-done = bf16[128,2048]{1,0:T(8,128)(2,1)} async-done(((bf16[512,2048]{1,0:T(8,128)(2,1)}), bf16[128,2048]{1,0:T(8,128)(2,1)}) %reduce-scatter.45.cloned.1.call-update) | async-done | bytes 524304
  858.8 10.7 while.38
  869.6 12.1 all-gather.30.cloned.1.call-done
  891.0 108.8 %while.39 = (s32[]{:T(128)}, f32[2,1024,2,64]{1,3,2,0:T(8,128)}, f32[2,1024,2,64]{1,3,2,0:T(8,128)S(1)}, bf16[2,2,512,2,64]{2,4,3,1,0:T(8,128)(2,1)}, bf16[2,2,5...) while((s32[]{:T(128)}, f32[2,1024,2,64]{1,3,2,0:T(8,128)}, ...), condition=%wide.region_54.55_spmd.clone, body=%wide.region_52.54_spmd.clone.sunk | while | flops 1387272192 | bytes 99673216 | solution.py:225
  891.2 4.5 fusion.786
  895.7 4.5 fusion.785
  900.2 18.7 %fusion.787 = f32[2,1024,2,64]{1,3,2,0:T(8,128)} fusion(f32[2,2,512,1024]{3,2,1,0:T(8,128)} %fusion.785, f32[2,2,512,1024]{3,2,1,0:T(8,128)} %fusion.786, f32[2,2,512]{2,1,0:T(2,128)S(1)} %dynamic-slice_bitcast_fusion.2, f32[2,1024,2,64]{1,3,2,0:T(8,128)} %get-tuple-element.705, pred[]{:T(512)S(6)} %compare.64, ...), kind=kOutput, calls=%fused_computation.48.clone.1 | convolution fusion | flops 287837184 | bytes 35930624 | tf_op jit(solution)/shard_map/while/body/eval_jaxpr/bhqk,bqhd->bkhd/dot_general | solution.py:219
  918.9 22.0 %fusion.789 = bf16[2,2,512,2,64]{2,4,3,1,0:T(8,128)(2,1)} fusion(bf16[2,2,512,2,64]{2,4,3,1,0:T(8,128)(2,1)} %get-tuple-element.707, s32[]{:T(128)} %get-tuple-element.704, bf16[2,1024,2,64]{1,3,2,0:T(8,128)(2,1)S(1)} %get-tuple-element.720, f32[2,2,512,1024]{3,2,1,0:T(8,128)} %fusion.785, f32[2,2,512,1024]{3,2,1,0:T(8,128)} %fusion.786, ...), kind=kOutput, calls=%fused_computation.51.clone.1 | convolution fusion | flops 287312896 | bytes 34619904 | tf_op jit(solution)/shard_map/while/body/eval_jaxpr/bhqk,bkhd->bqhd/dot_general | solution.py:216
  940.9 4.4 fusion.788
  945.4 4.5 fusion.786
  949.9 4.5 fusion.785
  954.4 18.9 %fusion.787 = f32[2,1024,2,64]{1,3,2,0:T(8,128)} fusion(f32[2,2,512,1024]{3,2,1,0:T(8,128)} %fusion.785, f32[2,2,512,1024]{3,2,1,0:T(8,128)} %fusion.786, f32[2,2,512]{2,1,0:T(2,128)S(1)} %dynamic-slice_bitcast_fusion.2, f32[2,1024,2,64]{1,3,2,0:T(8,128)} %get-tuple-element.705, pred[]{:T(512)S(6)} %compare.64, ...), kind=kOutput, calls=%fused_computation.48.clone.1 | convolution fusion | flops 287837184 | bytes 35930624 | tf_op jit(solution)/shard_map/while/body/eval_jaxpr/bhqk,bqhd->bkhd/dot_general | solution.py:219
  973.3 22.0 %fusion.789 = bf16[2,2,512,2,64]{2,4,3,1,0:T(8,128)(2,1)} fusion(bf16[2,2,512,2,64]{2,4,3,1,0:T(8,128)(2,1)} %get-tuple-element.707, s32[]{:T(128)} %get-tuple-element.704, bf16[2,1024,2,64]{1,3,2,0:T(8,128)(2,1)S(1)} %get-tuple-element.720, f32[2,2,512,1024]{3,2,1,0:T(8,128)} %fusion.785, f32[2,2,512,1024]{3,2,1,0:T(8,128)} %fusion.786, ...), kind=kOutput, calls=%fused_computation.51.clone.1 | convolution fusion | flops 287312896 | bytes 34619904 | tf_op jit(solution)/shard_map/while/body/eval_jaxpr/bhqk,bkhd->bqhd/dot_general | solution.py:216
  995.3 4.4 fusion.788
  1003.3 7.0 copy.152
  1010.3 8.3 convert_element_type.387
  1021.3 12.2 copy.262
  1033.5 12.1 reshape.855
  1045.7 31.5 %reduce-scatter.47.cloned.1.call-done = bf16[128,2048]{1,0:T(8,128)(2,1)} async-done(((bf16[512,2048]{1,0:T(8,128)(2,1)}), bf16[128,2048]{1,0:T(8,128)(2,1)}) %reduce-scatter.47.cloned.1.call-update) | async-done | bytes 524304
  1100.1 14.8 all-gather.32.cloned.1.call-done
  1137.9 6.2 psum.72
  1174.6 11.2 fusion.141
  1185.8 12.0 copy.264
  1197.8 12.1 reshape.857
  1274.4 58.3 %reduce-scatter.35.cloned.1.call-done = f32[1,128,506]{2,1,0:T(8,128)} async-done(((f32[1,1024,506]{2,1,0:T(8,128)}), f32[1,128,506]{2,1,0:T(8,128)}) %reduce-scatter.35.cloned.1.call-update) | async-done | bytes 259088 | tf_op jit(solution)/shard_map/reduce_scatter | solution.py:466
  1333.8 32.4 %reduce-scatter.49.cloned.1.call-done = bf16[128,2048]{1,0:T(8,128)(2,1)} async-done(((bf16[512,2048]{1,0:T(8,128)(2,1)}), bf16[128,2048]{1,0:T(8,128)(2,1)}) %reduce-scatter.49.cloned.1.call-update) | async-done | bytes 524304
  1372.3 65.5 %reduce-scatter.31.cloned.1.call-done = f32[2,128,256]{2,1,0:T(8,128)} async-done(((f32[2,1024,256]{2,1,0:T(8,128)}), f32[2,128,256]{2,1,0:T(8,128)}) %reduce-scatter.31.cloned.1.call-update) | async-done | bytes 262160 | tf_op jit(solution)/shard_map/reduce_scatter | solution.py:463
  1440.9 96.1 %reduce-scatter.29.cloned.1.call-done = f32[2,576,128]{2,1,0:T(8,128)} async-done(((f32[2,4608,128]{2,1,0:T(8,128)}), f32[2,576,128]{2,1,0:T(8,128)}) %reduce-scatter.29.cloned.1.call-update) | async-done | bytes 589840 | tf_op jit(solution)/shard_map/reduce_scatter | solution.py:462
  1538.5 130.9 %reduce-scatter.27.cloned.1.call-done = f32[3,576,128]{2,1,0:T(8,128)} async-done(((f32[3,4608,128]{2,1,0:T(8,128)}), f32[3,576,128]{2,1,0:T(8,128)}) %reduce-scatter.27.cloned.1.call-update) | async-done | bytes 884752 | tf_op jit(solution)/shard_map/reduce_scatter | solution.py:461
  1671.1 10.7 psum.73
  1686.5 29.5 %all-reduce.63 = (f32[2436]{0:T(1024)S(1)}, f32[6,2,128]{2,1,0:T(2,128)S(1)}) all-reduce(f32[2436]{0:T(1024)S(1)} %concatenate.49, f32[6,2,128]{2,1,0:T(2,128)S(1)} %constant_dynamic-update-slice_fusion), channel_id=1, replica_groups=mesh['dp'=8,'chan'=4] {'dp'}, use_global_device_ids=true, to_apply=%region_94.95 | all-reduce | flops 3972 | bytes 31776 | tf_op jit(solution)/shard_map/psum | solution.py:502
  1734.1 47.1 %all-reduce.62 = (f32[]{:T(128)}, f32[10]{0:T(128)}, f32[10]{0:T(128)}, f32[6,2]{1,0:T(8,128)}, f32[6,2]{1,0:T(8,128)}) all-reduce(f32[]{:T(128)S(6)} %div.439, f32[10]{0:T(128)} %concatenate.51, f32[10]{0:T(128)} %concatenate.50, f32[6,2]{1,0:T(8,128)} %broadcast_multiply_fusion, ...), channel_id=1, replica_groups=mesh['dp'=8,'chan'=4] {'dp','chan'}, use_global_device_ids=true, to_apply=%region_33.34 | all-reduce | flops 45 | bytes 360 | tf_op jit(solution)/shard_map/psum | solution.py:525
  (797 shorter events, 462.6 us)
Async XLA Ops:
  7.2 83.6 %all-gather.18.cloned.1.call-start = ((), (), s32[]{:S(2)}) async-start(), calls=%async_computation.14 | async-start | bytes 1179648 | tf_op jit(solution)/shard_map/all_gather | solution.py:387
  9.6 84.0 %all-gather.14.cloned.1.call-start = ((), (), s32[]{:S(2)}) async-start(), calls=%async_computation.12 | async-start | bytes 2621440 | tf_op jit(solution)/shard_map/all_gather | solution.py:35
  14.1 145.9 %copy-start.105 = (f32[128]{0:T(128)}, f32[128]{0:T(128)S(1)}, u32[]{:S(2)}) copy-start(f32[128]{0:T(128)S(1)} %get-tuple-element.493) | copy-start | bytes 1540
  14.2 145.9 %copy-start.117 = (f32[128]{0:T(128)}, f32[128]{0:T(128)S(1)}, u32[]{:S(2)}) copy-start(f32[128]{0:T(128)S(1)} %get-tuple-element.492) | copy-start | bytes 1540
  14.2 283.4 %copy-start.83 = (f32[128]{0:T(128)}, f32[128]{0:T(128)S(1)}, u32[]{:S(2)}) copy-start(f32[128]{0:T(128)S(1)} %get-tuple-element.491) | copy-start | bytes 1540
  16.5 126.9 %all-gather.16.cloned.1.call-start = ((), (), s32[]{:S(2)}) async-start(), calls=%async_computation.13 | async-start | bytes 3981312 | tf_op jit(solution)/shard_map/all_gather | solution.py:385
  18.0 178.9 %all-gather.20.cloned.1.call-start = ((), (), s32[]{:S(2)}) async-start(), calls=%async_computation.15 | async-start | bytes 2654208 | tf_op jit(solution)/shard_map/all_gather | solution.py:386
  19.5 270.2 %reduce-scatter.37.cloned.1.call-start = ((), (), s32[]{:S(2)}) async-start(), calls=%async_computation.27 | async-start | bytes 2621440
  90.7 336.9 %copy-start.56 = (f32[2,1024]{1,0:T(2,128)}, f32[2,1024]{1,0:T(2,128)S(1)}, u32[]{:S(2)}) copy-start(f32[2,1024]{1,0:T(2,128)S(1)} %psum.70) | copy-start | bytes 24580
  258.7 70.3 %all-gather.22.cloned.1.call-start = ((), (), s32[]{:S(2)}) async-start(), calls=%async_computation.16 | async-start | bytes 2621440 | tf_op jit(solution)/shard_map/all_gather | solution.py:35
  296.5 127.9 %copy-start.21 = (bf16[2,32,32,128]{3,2,1,0:T(8,128)(2,1)}, bf16[2,32,32,128]{3,2,1,0:T(8,128)(2,1)S(1)}, u32[]{:S(2)}) copy-start(bf16[2,32,32,128]{3,2,1,0:T(8,128)(2,1)S(1)} %copy.253) | copy-start | bytes 1572868
  298.7 119.0 %reduce-scatter.39.cloned.1.call-start = ((), (), s32[]{:S(2)}) async-start(), calls=%async_computation.28 | async-start | bytes 2621440
  384.0 65.7 %all-gather.24.cloned.1.call-start = ((), (), s32[]{:S(2)}) async-start(), calls=%async_computation.17 | async-start | bytes 2621440 | tf_op jit(solution)/shard_map/all_gather | solution.py:35
  426.7 135.2 %reduce-scatter.41.cloned.1.call-start = ((), (), s32[]{:S(2)}) async-start(), calls=%async_computation.29 | async-start | bytes 2621440
  530.3 63.7 %all-gather.26.cloned.1.call-start = ((), (), s32[]{:S(2)}) async-start(), calls=%async_computation.18 | async-start | bytes 2621440 | tf_op jit(solution)/shard_map/all_gather | solution.py:35
  571.0 121.5 %reduce-scatter.43.cloned.1.call-start = ((), (), s32[]{:S(2)}) async-start(), calls=%async_computation.30 | async-start | bytes 2621440
  660.9 67.2 %all-gather.28.cloned.1.call-start = ((), (), s32[]{:S(2)}) async-start(), calls=%async_computation.19 | async-start | bytes 2621440 | tf_op jit(solution)/shard_map/all_gather | solution.py:51
  702.9 153.1 %copy-start.77 = (f32[2,128]{1,0:T(2,128)}, f32[2,128]{1,0:T(2,128)S(1)}, u32[]{:S(2)}) copy-start(f32[2,128]{1,0:T(2,128)S(1)} %broadcast_in_dim.243) | copy-start | bytes 3076
  705.1 140.5 %reduce-scatter.45.cloned.1.call-start = ((), (), s32[]{:S(2)}) async-start(), calls=%async_computation.31 | async-start | bytes 2621440
  814.0 67.7 %all-gather.30.cloned.1.call-start = ((), (), s32[]{:S(2)}) async-start(), calls=%async_computation.20 | async-start | bytes 2621440 | tf_op jit(solution)/shard_map/all_gather | solution.py:51
  858.7 218.5 %reduce-scatter.47.cloned.1.call-start = ((), (), s32[]{:S(2)}) async-start(), calls=%async_computation.32 | async-start | bytes 2621440
  1045.7 69.3 %all-gather.32.cloned.1.call-start = ((), (), s32[]{:S(2)}) async-start(), calls=%async_computation.21 | async-start | bytes 2621440 | tf_op jit(solution)/shard_map/all_gather | solution.py:51
  1091.9 180.0 %all-reduce.66.cloned.1.call-start = ((), (), s32[]{:S(2)}) async-start(), calls=%async_computation.34 | async-start | bytes 2097152
  1099.6 173.8 %reduce-scatter.33.cloned.1.call-start = ((), (), s32[]{:S(2)}) async-start(), calls=%async_computation.25 | async-start | bytes 294912 | tf_op jit(solution)/shard_map/reduce_scatter | solution.py:465
  1145.2 187.5 %reduce-scatter.35.cloned.1.call-start = ((), (), s32[]{:S(2)}) async-start(), calls=%async_computation.26 | async-start | bytes 2359296 | tf_op jit(solution)/shard_map/reduce_scatter | solution.py:466
  1147.1 219.1 %reduce-scatter.49.cloned.1.call-start = ((), (), s32[]{:S(2)}) async-start(), calls=%async_computation.33 | async-start | bytes 2621440
  1209.9 227.8 %reduce-scatter.31.cloned.1.call-start = ((), (), s32[]{:S(2)}) async-start(), calls=%async_computation.24 | async-start | bytes 2359296 | tf_op jit(solution)/shard_map/reduce_scatter | solution.py:463
  1223.7 313.3 %reduce-scatter.29.cloned.1.call-start = ((), (), s32[]{:S(2)}) async-start(), calls=%async_computation.23 | async-start | bytes 5308416 | tf_op jit(solution)/shard_map/reduce_scatter | solution.py:462
  1238.4 430.9 %reduce-scatter.27.cloned.1.call-start = ((), (), s32[]{:S(2)}) async-start(), calls=%async_computation.22 | async-start | bytes 7962624 | tf_op jit(solution)/shard_map/reduce_scatter | solution.py:461
  1273.5 450.2 %copy-start.51 = (f32[1,64,512]{2,0,1:T(1,128)}, f32[1,64,512]{2,0,1:T(1,128)S(1)}, u32[]{:S(2)}) copy-start(f32[1,64,512]{2,0,1:T(1,128)S(1)} %get-tuple-element.446) | copy-start | bytes 393220
  1333.8 105.2 %copy-start.20 = (bf16[2,32,32,128]{3,2,1,0:T(8,128)(2,1)S(1)}, bf16[2,32,32,128]{3,2,1,0:T(8,128)(2,1)}, u32[]{:S(2)}) copy-start(bf16[2,32,32,128]{3,2,1,0:T(8,128)(2,1)} %param.31) | copy-start | bytes 1572868
  1333.8 105.2 %copy-start.74 = (f32[2,128]{1,0:T(2,128)S(1)}, f32[2,128]{1,0:T(2,128)}, u32[]{:S(2)}) copy-start(f32[2,128]{1,0:T(2,128)} %copy-done.73) | copy-start | bytes 3076
  1333.8 105.2 %copy-start.101 = (f32[2,128]{1,0:T(2,128)S(1)}, f32[2,128]{1,0:T(2,128)}, u32[]{:S(2)}) copy-start(f32[2,128]{1,0:T(2,128)} %copy-done.100) | copy-start | bytes 3076
  1333.8 105.2 %copy-start.110 = (f32[128]{0:T(128)S(1)}, f32[128]{0:T(128)}, u32[]{:S(2)}) copy-start(f32[128]{0:T(128)} %copy-done.109) | copy-start | bytes 1540
  1333.8 105.2 %copy-start.112 = (f32[128]{0:T(128)S(1)}, f32[128]{0:T(128)}, u32[]{:S(2)}) copy-start(f32[128]{0:T(128)} %copy-done.111) | copy-start | bytes 1540
  1369.2 71.5 %copy-start.141 = (f32[128]{0:T(128)S(1)}, f32[128]{0:T(128)}, u32[]{:S(2)}) copy-start(f32[128]{0:T(128)} %get-tuple-element.339) | copy-start | bytes 1540
  1369.2 71.5 %copy-start.142 = (f32[128]{0:T(128)S(1)}, f32[128]{0:T(128)}, u32[]{:S(2)}) copy-start(f32[128]{0:T(128)} %get-tuple-element.352) | copy-start | bytes 1540
  1369.2 71.5 %copy-start.133 = (f32[128]{0:T(128)S(1)}, f32[128]{0:T(128)}, u32[]{:S(2)}) copy-start(f32[128]{0:T(128)} %get-tuple-element.361) | copy-start | bytes 1540
  1369.2 71.5 %copy-start.134 = (f32[128]{0:T(128)S(1)}, f32[128]{0:T(128)}, u32[]{:S(2)}) copy-start(f32[128]{0:T(128)} %get-tuple-element.349) | copy-start | bytes 1540
  1369.3 71.5 %copy-start.131 = (f32[128]{0:T(128)S(1)}, f32[128]{0:T(128)}, u32[]{:S(2)}) copy-start(f32[128]{0:T(128)} %get-tuple-element.346) | copy-start | bytes 1540
  1369.3 71.5 %copy-start.132 = (f32[128]{0:T(128)S(1)}, f32[128]{0:T(128)}, u32[]{:S(2)}) copy-start(f32[128]{0:T(128)} %get-tuple-element.347) | copy-start | bytes 1540
  1369.3 71.5 %copy-start.139 = (f32[128]{0:T(128)S(1)}, f32[128]{0:T(128)}, u32[]{:S(2)}) copy-start(f32[128]{0:T(128)} %get-tuple-element.337) | copy-start | bytes 1540
  1369.3 71.5 %copy-start.140 = (f32[128]{0:T(128)S(1)}, f32[128]{0:T(128)}, u32[]{:S(2)}) copy-start(f32[128]{0:T(128)} %get-tuple-element.351) | copy-start | bytes 1540
  1369.3 71.5 %copy-start.129 = (f32[128]{0:T(128)S(1)}, f32[128]{0:T(128)}, u32[]{:S(2)}) copy-start(f32[128]{0:T(128)} %get-tuple-element.343) | copy-start | bytes 1540
  1369.3 71.5 %copy-start.130 = (f32[128]{0:T(128)S(1)}, f32[128]{0:T(128)}, u32[]{:S(2)}) copy-start(f32[128]{0:T(128)} %get-tuple-element.344) | copy-start | bytes 1540
  1369.3 312.7 %copy-start.143 = (f32[2,128]{1,0:T(2,128)S(1)}, f32[2,128]{1,0:T(2,128)}, u32[]{:S(2)}) copy-start(f32[2,128]{1,0:T(2,128)} %param.47) | copy-start | bytes 3076
  1369.3 312.9 %copy-start.147 = (f32[64]{0:T(128)S(1)}, f32[64]{0:T(128)}, u32[]{:S(2)}) copy-start(f32[64]{0:T(128)} %param.49) | copy-start | bytes 772
  1369.3 313.6 %copy-start.148 = (f32[32]{0:T(128)S(1)}, f32[32]{0:T(128)}, u32[]{:S(2)}) copy-start(f32[32]{0:T(128)} %param.51) | copy-start | bytes 388
  1369.4 314.2 %copy-start.149 = (f32[128]{0:T(128)S(1)}, f32[128]{0:T(128)}, u32[]{:S(2)}) copy-start(f32[128]{0:T(128)} %param.53) | copy-start | bytes 1540
  1369.4 314.8 %copy-start.85 = (f32[3,576]{1,0:T(4,128)S(1)}, f32[3,576]{1,0:T(4,128)}, u32[]{:S(2)}) copy-start(f32[3,576]{1,0:T(4,128)} %param.43) | copy-start | bytes 20740
  1369.4 314.9 %copy-start.108 = (f32[2,576]{1,0:T(2,128)S(1)}, f32[2,576]{1,0:T(2,128)}, u32[]{:S(2)}) copy-start(f32[2,576]{1,0:T(2,128)} %param.45) | copy-start | bytes 13828
  1369.4 347.3 %copy-start.135 = (f32[506]{0:T(512)S(1)}, f32[506]{0:T(512)}, u32[]{:S(2)}) copy-start(f32[506]{0:T(512)} %param.54) | copy-start | bytes 6076
  1369.4 347.9 %copy-start.144 = (f32[256]{0:T(256)S(1)}, f32[256]{0:T(256)}, u32[]{:S(2)}) copy-start(f32[256]{0:T(256)} %param.52) | copy-start | bytes 3076
  1369.4 348.4 %copy-start.136 = (f32[512]{0:T(512)S(1)}, f32[512]{0:T(512)}, u32[]{:S(2)}) copy-start(f32[512]{0:T(512)} %param.50) | copy-start | bytes 6148
  1369.4 349.0 %copy-start.145 = (f32[2,128]{1,0:T(2,128)S(1)}, f32[2,128]{1,0:T(2,128)}, u32[]{:S(2)}) copy-start(f32[2,128]{1,0:T(2,128)} %param.46) | copy-start | bytes 3076
  1369.4 349.6 %copy-start.137 = (f32[3,128]{1,0:T(4,128)S(1)}, f32[3,128]{1,0:T(4,128)}, u32[]{:S(2)}) copy-start(f32[3,128]{1,0:T(4,128)} %param.44) | copy-start | bytes 4612
  1369.5 350.2 %copy-start.107 = (f32[6,2,128]{2,1,0:T(2,128)S(1)}, f32[6,2,128]{2,1,0:T(2,128)}, u32[]{:S(2)}) copy-start(f32[6,2,128]{2,1,0:T(2,128)} %param.55) | copy-start | bytes 18436
  1369.5 353.4 %copy-start.138 = (f32[2,256]{1,0:T(2,128)S(1)}, f32[2,256]{1,0:T(2,128)}, u32[]{:S(2)}) copy-start(f32[2,256]{1,0:T(2,128)} %param.48) | copy-start | bytes 6148
  1372.3 352.9 %copy-start.47 = (f32[1,128,506]{2,1,0:T(8,128)S(1)}, f32[1,128,506]{2,1,0:T(8,128)}, u32[]{:S(2)}) copy-start(f32[1,128,506]{2,1,0:T(8,128)} %reduce-scatter.35.cloned.1.call-done) | copy-start | bytes 777220
  1372.3 353.8 %copy-start.55 = (f32[1,32,256]{2,1,0:T(8,128)S(1)}, f32[1,32,256]{2,1,0:T(8,128)}, u32[]{:S(2)}) copy-start(f32[1,32,256]{2,1,0:T(8,128)} %reduce-scatter.33.cloned.1.call-done) | copy-start | bytes 98308
  1437.8 289.0 %copy-start.48 = (f32[2,128,256]{2,1,0:T(8,128)S(1)}, f32[2,128,256]{2,1,0:T(8,128)}, u32[]{:S(2)}) copy-start(f32[2,128,256]{2,1,0:T(8,128)} %reduce-scatter.31.cloned.1.call-done) | copy-start | bytes 786436
  1537.0 190.5 %copy-start.39 = (f32[2,576,128]{2,1,0:T(8,128)S(1)}, f32[2,576,128]{2,1,0:T(8,128)}, u32[]{:S(2)}) copy-start(f32[2,576,128]{2,1,0:T(8,128)} %reduce-scatter.29.cloned.1.call-done) | copy-start | bytes 1769476
  1670.9 123.0 %copy-start.59 = (f32[32,256]{1,0:T(8,128)S(1)}, f32[32,256]{1,0:T(8,128)}, u32[]{:S(2)}) copy-start(f32[32,256]{1,0:T(8,128)} %param.40) | copy-start | bytes 98308
  1725.2 71.9 %copy-start.46 = (f32[2,576,128]{2,1,0:T(8,128)S(1)}, f32[2,576,128]{2,1,0:T(8,128)}, u32[]{:S(2)}) copy-start(f32[2,576,128]{2,1,0:T(8,128)} %param.37) | copy-start | bytes 1769476
  (117 other events, 1709.4 us)
Sparse Core Ops, SparseCore 0:
  10.8 40.6 all-gather.17
  53.6 22.8 all-gather.13
  79.3 64.1 all-gather.15
  146.1 50.8 all-gather.19
  258.8 30.8 reduce-scatter.36
  298.8 22.8 all-gather.21
  384.2 33.4 reduce-scatter.38
  426.8 22.8 all-gather.23
  530.4 31.4 reduce-scatter.40
  571.1 22.8 all-gather.25
  661.0 31.4 reduce-scatter.42
  705.2 22.8 all-gather.27
  814.1 31.4 reduce-scatter.44
  858.8 22.8 all-gather.29
  1045.7 31.4 reduce-scatter.46
  1092.1 22.8 all-gather.31
  1118.3 77.5 all-reduce.65
  1200.6 61.1 reduce-scatter.32
  1266.3 66.3 reduce-scatter.34
  1335.2 30.9 reduce-scatter.48
  1370.4 67.3 reduce-scatter.30
  1442.0 94.9 reduce-scatter.28
  1541.2 128.0 reduce-scatter.26
where the time goes:
time: 1810 us
  waiting for transfers between devices  755 us (42%)
  matrix products  457 us (25%)
  local copies, waits for them, and re-layouts  283 us (16%)
  blocking collectives  191 us (11%)
  other arithmetic  92.7 us (5%)
  between operations  24.2 us (1%)
    unnamed x349, local copies, waits for them, and re-layouts  230 us
    unnamed x31, waiting for transfers between devices  223 us
    reduce_scatter x1, waiting for transfers between devices, per_device(): lax.psum_scatter(local_grads[0], 'dp', scatter_dimension=1, tiled=True)  131 us
    dot_general x27, matrix products, conv_gathered_back(): jnp.einsum('bhwo,io->bhwi', grad_out, kernel_tap, preferred_element_type=...  109 us
    reduce_scatter x1, waiting for transfers between devices, per_device(): lax.psum_scatter(local_grads[1], 'dp', scatter_dimension=1, tiled=True)  96.1 us
    dot_general x18, matrix products, conv_split(): jnp.einsum('bhwi,oi->bhwo', local_in, kernel_tap, preferred_element_type=...  76.8 us
    reduce_scatter x1, waiting for transfers between devices, per_device(): lax.psum_scatter(local_grads[2], 'dp', scatter_dimension=1, tiled=True)  65.5 us
    reduce_scatter x1, waiting for transfers between devices, per_device(): lax.psum_scatter(local_grads[5], 'dp', scatter_dimension=1, tiled=True)  58.3 us
  transfers between devices with their start and end apart: 23, of which 18 were waited for; matrix products, arithmetic and copies ran while one was open for 11% of the time, Pallas kernels for 0%

commit v1 on v0

v1 whole, which is shorter than its diff:
```python
import functools
import math

import jax
import jax.numpy as jnp
from jax import lax
from jax.experimental import pallas as pl
from jax.experimental.pallas import tpu as pltpu
from jax.sharding import Mesh
from jax.sharding import PartitionSpec as P

C = 512
HEADS = 8
GROUPS = 32
TF = 256
STEP = 10
SIDE = 32
PIX = 1024
HALF = 256
BLOCK = 128
PAD = SIDE
ROWS = PIX + 2 * PAD
CHUNK = 256

single = jnp.float32
narrow = jnp.bfloat16
step_rate = 0.5
floor_scale = 0.001
tiny_square = 1e-30
norm_eps = 1e-05

TAPS = [(t // 3 - 1, t % 3 - 1) for t in range(9)]


def dot(a, b):
    return jnp.dot(a, b, preferred_element_type=single)


def dot_t(a, b):
    return lax.dot_general(a, b, (((1,), (1,)), ((), ())), preferred_element_type=single)


def group_sum(row):
    lane = lax.broadcasted_iota(jnp.int32, (HALF, HALF), 0)
    other = lax.broadcasted_iota(jnp.int32, (HALF, HALF), 1)
    size = C // GROUPS
    ones = jnp.where(lane // size == other // size, 1.0, 0.0).astype(single)
    tall = jnp.broadcast_to(row, (8, HALF))
    return jnp.dot(tall, ones, precision=lax.Precision.HIGHEST, preferred_element_type=single)[0:1]


def loop_sum(count, make):
    zeros = make(None)

    def body(i, carried):
        return [old + new for old, new in zip(carried, make(i))]

    return lax.fori_loop(0, count, body, [jnp.zeros((1, HALF), single)] * zeros)


def rows_of(i, size=CHUNK, offset=0):
    return pl.ds(pl.multiple_of(offset + i * size, 32), size)


def stats(x_ref):
    members = float(PIX * (C // GROUPS))

    def first(i):
        if i is None:
            return 1
        return [jnp.sum(x_ref[rows_of(i), :], 0, keepdims=True)]

    (total,) = loop_sum(PIX // CHUNK, first)
    mean = group_sum(total) / members

    def second(i):
        if i is None:
            return 1
        center = x_ref[rows_of(i), :] - mean
        return [jnp.sum(center * center, 0, keepdims=True)]

    (square,) = loop_sum(PIX // CHUNK, second)
    rstd = lax.rsqrt(group_sum(square) / members + norm_eps)
    return mean, rstd


def sigmoid(v):
    return 1.0 / (1.0 + jnp.exp(-v))


def norm_forward(x_ref, gain, bias, act, store):
    mean, rstd = stats(x_ref)

    @pl.loop(0, PIX // CHUNK)
    def _(i):
        value = (x_ref[rows_of(i), :] - mean) * rstd * gain + bias
        if act:
            value = value * sigmoid(value)
        store(i, value.astype(narrow))


def norm_backward(x_ref, load_grad, gain, bias, act, tmp_ref, store):
    mean, rstd = stats(x_ref)
    members = float(PIX * (C // GROUPS))

    def first(i):
        if i is None:
            return 2
        hat = (x_ref[rows_of(i), :] - mean) * rstd
        grad = load_grad(i)
        if act:
            mixed = hat * gain + bias
            gate = sigmoid(mixed)
            grad = grad * gate * (1.0 + mixed * (1.0 - gate))
        tmp_ref[rows_of(i), :] = grad
        return [jnp.sum(grad, 0, keepdims=True), jnp.sum(grad * hat, 0, keepdims=True)]

    total, along = loop_sum(PIX // CHUNK, first)
    mean_grad = group_sum(gain * total) / members
    mean_along = group_sum(gain * along) / members

    @pl.loop(0, PIX // CHUNK)
    def _(i):
        hat = (x_ref[rows_of(i), :] - mean) * rstd
        store(i, rstd * (tmp_ref[rows_of(i), :] * gain - mean_grad - hat * mean_along))

    return total, along


def shifts(load, s_ref, width):
    for b in range(3):
        s_ref[b, 0:PAD, 0:width] = jnp.zeros((PAD, width), narrow)
        s_ref[b, PAD + PIX : ROWS, 0:width] = jnp.zeros((PAD, width), narrow)
    size = 128

    @pl.loop(0, PIX // size)
    def _(i):
        value = load(i, size)
        wide = value.astype(single)
        across = lax.broadcasted_iota(jnp.int32, wide.shape, 0) % SIDE
        left = jnp.where(across > 0, pltpu.roll(wide, 1, 0), 0.0)
        right = jnp.where(across < SIDE - 1, pltpu.roll(wide, size - 1, 0), 0.0)
        at = rows_of(i, size, PAD)
        s_ref[0, at, 0:width] = left.astype(narrow)
        s_ref[1, at, 0:width] = value
        s_ref[2, at, 0:width] = right.astype(narrow)


def tap_rows(s_ref, t, sign, i, size, width):
    a, b = TAPS[t]
    return s_ref[sign * b + 1, rows_of(i, size, PAD + sign * a * SIDE), 0:width]


def split_core(value):
    core = lax.axis_index("lo")
    b0, b1, b2, b3 = [value[:, k * BLOCK : (k + 1) * BLOCK] for k in range(4)]
    even, odd = jnp.concatenate([b0, b2], 1), jnp.concatenate([b1, b3], 1)
    first = core == 0
    return jnp.where(first, even, odd), jnp.where(first, odd, even)


def join_core(own_ref, peer_ref, full_ref):
    core = lax.axis_index("lo")

    @pl.loop(0, PIX // CHUNK)
    def _(i):
        at = rows_of(i)
        own, peer = own_ref[at, :].astype(single), peer_ref[at, :].astype(single)
        even = jnp.where(core == 0, own, peer).astype(narrow)
        odd = jnp.where(core == 0, peer, own).astype(narrow)
        full_ref[at, 0:BLOCK] = even[:, 0:BLOCK]
        full_ref[at, BLOCK : 2 * BLOCK] = odd[:, 0:BLOCK]
        full_ref[at, 2 * BLOCK : 3 * BLOCK] = even[:, BLOCK:]
        full_ref[at, 3 * BLOCK :] = odd[:, BLOCK:]


def conv_wide(s_ref, w_ref, store):
    @pl.loop(0, PIX // CHUNK)
    def _(i):
        total = None
        for t in range(9):
            part = dot(tap_rows(s_ref, t, 1, i, CHUNK, C), w_ref[t * C : (t + 1) * C, :])
            total = part if total is None else total + part
        store(i, total)


def conv_tall(s_ref, w_ref, sign, store):
    @pl.loop(0, PIX // CHUNK)
    def _(i):
        total = None
        for t in range(9):
            part = dot_t(tap_rows(s_ref, t, sign, i, CHUNK, HALF), w_ref[t * C : (t + 1) * C, :])
            total = part if total is None else total + part
        store(i, total)


def conv_back(s_ref, w_ref, store):
    @pl.loop(0, PIX // CHUNK)
    def _(i):
        total = None
        for t in range(9):
            part = dot(tap_rows(s_ref, t, -1, i, CHUNK, C), w_ref[t * C : (t + 1) * C, :])
            total = part if total is None else total + part
        store(i, total)


def transpose_into(load, t_ref):
    for i in range(PIX // CHUNK):
        t_ref[:, i * CHUNK : (i + 1) * CHUNK] = jnp.transpose(load(i).astype(single)).astype(narrow)


def kernel_grad(t_ref, s_ref, sign, store):
    for t in range(9):
        a, b = TAPS[t]
        start = PAD + sign * a * SIDE
        store(t, dot(t_ref[...], s_ref[sign * b + 1, start : start + PIX, 0:HALF]))


def low_lanes(shape):
    return lax.broadcasted_iota(jnp.int32, shape, 1) < BLOCK // 2


def swap_halves(value):
    half = BLOCK // 2
    return jnp.concatenate([value[:, half:], value[:, :half]], 1)


def mask_half(value, upper):
    low = low_lanes(value.shape)
    return jnp.where(low != upper, value.astype(single), 0.0).astype(narrow)


def head_parts(qkv_ref, s, h):
    base = 3 * BLOCK * s
    b0, b1, b2 = [slice(base + k * BLOCK, base + (k + 1) * BLOCK) for k in range(3)]
    return (b0, b0, b1) if h == 0 else (b1, b2, b2)


SCALE = (C // HEADS) ** (-0.5)


def attend(qkv_ref, k_ref, vt_ref, log_ref, out_ref):
    for s in range(2):
        for h in range(2):
            q_at, k_at, v_at = head_parts(qkv_ref, s, h)
            k_ref[...] = swap_halves(qkv_ref[:, k_at])
            vt_ref[...] = jnp.transpose(qkv_ref[:, v_at].astype(single)).astype(narrow)

            @pl.loop(0, PIX // CHUNK)
            def _(i):
                query = mask_half(qkv_ref[rows_of(i), q_at], h == 1)
                scores = dot_t(k_ref[...], query) * SCALE
                top = jnp.max(scores, 0, keepdims=True)
                exponent = jnp.exp(scores - top)
                total = jnp.sum(exponent, 0, keepdims=True)
                mixed = dot(vt_ref[...], exponent.astype(narrow)) / total
                log_ref[2 * s + h, i] = top + jnp.log(total)
                turned = jnp.transpose(mixed)
                at = rows_of(i)
                lanes = slice(s * BLOCK, (s + 1) * BLOCK)
                if h == 0:
                    out_ref[at, lanes] = turned.astype(narrow)
                else:
                    kept = out_ref[at, lanes].astype(single)
                    out_ref[at, lanes] = jnp.where(low_lanes(turned.shape), kept, turned).astype(narrow)


def attend_back(qkv_ref, log_ref, grad_ref, k_ref, kt_ref, dk_ref, dv_ref, dqkv):
    for s in range(2):
        lanes = slice(s * BLOCK, (s + 1) * BLOCK)
        for h in range(2):
            q_at, k_at, v_at = head_parts(qkv_ref, s, h)
            q_to, k_to, v_to = head_parts(None, 0, h)
            grad_to = dqkv[s]
            k_ref[...] = swap_halves(qkv_ref[:, k_at])
            kt_ref[...] = jnp.transpose(k_ref[...].astype(single)).astype(narrow)
            dk_ref[...] = jnp.zeros_like(dk_ref)
            dv_ref[...] = jnp.zeros_like(dv_ref)

            @pl.loop(0, PIX // CHUNK)
            def _(i):
                at = rows_of(i)
                query = mask_half(qkv_ref[at, q_at], h == 1)
                grad = mask_half(grad_ref[at, lanes], h == 1)
                weights = jnp.exp(dot_t(k_ref[...], query) * SCALE - log_ref[2 * s + h, i])
                dv_ref[...] += dot(weights.astype(narrow), grad)
                dweights = dot_t(qkv_ref[:, v_at], grad)
                inner = jnp.sum(weights * dweights, 0, keepdims=True)
                dscores = (weights * (dweights - inner) * SCALE).astype(narrow)
                dk_ref[...] += dot(dscores, query)
                turned = jnp.transpose(dot(kt_ref[...], dscores))
                kept = grad_to[at, q_to].astype(single)
                low = low_lanes(turned.shape)
                if h == 0:
                    grad_to[at, q_to] = turned.astype(narrow)
                else:
                    grad_to[at, q_to] = jnp.where(low, kept, turned).astype(narrow)

            low = low_lanes((PIX, BLOCK))
            dk = swap_halves(dk_ref[...])
            if h == 0:
                grad_to[:, k_to] = jnp.where(low, grad_to[:, k_to].astype(single), dk).astype(narrow)
                grad_to[:, v_to] = dv_ref[...].astype(narrow)
            else:
                grad_to[:, k_to] = jnp.where(low, dk, dv_ref[...]).astype(narrow)


VMEM = pl.BlockSpec(memory_space=pltpu.VMEM)


def call(body, outs, scratch, args, name):
    return pl.pallas_call(
        body,
        out_shape=outs,
        in_specs=[VMEM] * len(args),
        out_specs=[VMEM] * len(outs),
        scratch_shapes=scratch,
        compiler_params=pltpu.CompilerParams(vmem_limit_bytes=56 * 2**20),
        name=name,
    )(*args)


def struct(shape, dtype=single):
    return jax.ShapeDtypeStruct(shape, dtype)


def entry_kernel(act, x_ref, own_ref, recv_ref, norm_ref, stream_ref, entry_ref):
    @pl.loop(0, PIX // CHUNK)
    def _(i):
        at = rows_of(i)
        stream_ref[at, :] = x_ref[at, :] + (own_ref[at, :] + recv_ref[at, :].astype(single))

    def store(i, value):
        entry_ref[rows_of(i), :] = value

    norm_forward(stream_ref, norm_ref[0:1, :], norm_ref[1:2, :], act, store)


def first_kernel(x_ref, norm_ref, stream_ref, entry_ref):
    @pl.loop(0, PIX // CHUNK)
    def _(i):
        at = rows_of(i)
        stream_ref[at, :] = x_ref[at, :].astype(single)

    def store(i, value):
        entry_ref[rows_of(i), :] = value

    norm_forward(stream_ref, norm_ref[0:1, :], norm_ref[1:2, :], True, store)


def mid_rows(norm_ref, mod_ref):
    gain, bias = norm_ref[0:1, :], norm_ref[1:2, :]
    scale, shift = 1.0 + mod_ref[0:1, :], mod_ref[1:2, :]
    return gain, bias, scale, shift


def put_split(own_ref, peer_ref):
    def store(i, value):
        own, peer = split_core(value)
        own_ref[rows_of(i), :] = own
        peer_ref[rows_of(i), :] = peer.astype(narrow)

    return store


def shift_full(full_ref, s_ref, width):
    shifts(lambda i, size: full_ref[rows_of(i, size), :], s_ref, width)


def res_kernel(own_ref, peer_ref, win_ref, wout_ref, norm_ref, mod_ref, inner_ref, hidden_ref, part_ref, send_ref, full_ref, s_ref):
    join_core(own_ref, peer_ref, full_ref)
    shift_full(full_ref, s_ref, C)

    def put(i, value):
        inner_ref[rows_of(i), :] = value

    conv_wide(s_ref, win_ref, put)
    gain, bias, scale, shift = mid_rows(norm_ref, mod_ref)

    def store(i, value):
        hidden_ref[rows_of(i), :] = value

    norm_forward(inner_ref, gain * scale, bias * scale + shift, True, store)
    shift_full(hidden_ref, s_ref, HALF)
    conv_tall(s_ref, wout_ref, 1, put_split(part_ref, send_ref))


def attn_kernel(own_ref, peer_ref, w_ref, qkv_ref, log_ref, out_ref, part_ref, send_ref, full_ref, k_ref, vt_ref):
    join_core(own_ref, peer_ref, full_ref)

    @pl.loop(0, PIX // CHUNK)
    def _(i):
        at = rows_of(i)
        for s in range(2):
            value = dot(full_ref[at, :], w_ref[:, s * C : s * C + 3 * BLOCK])
            qkv_ref[at, s * 3 * BLOCK : (s + 1) * 3 * BLOCK] = value.astype(narrow)

    attend(qkv_ref, k_ref, vt_ref, log_ref, out_ref)
    store = put_split(part_ref, send_ref)

    @pl.loop(0, PIX // CHUNK)
    def _(i):
        at = rows_of(i)
        value = dot_t(out_ref[at, 0:BLOCK], w_ref[:, 3 * BLOCK : C])
        store(i, value + dot_t(out_ref[at, BLOCK:], w_ref[:, C + 3 * BLOCK :]))


def load_rows(ref):
    return lambda i: ref[rows_of(i), :]


def head_kernel(total, own_ref, peer_ref, w_ref, noise_ref, weight_ref, loss_ref, dw_ref, part_ref, send_ref, full_ref, s_ref, t_ref, grad_ref):
    join_core(own_ref, peer_ref, full_ref)
    shift_full(full_ref, s_ref, C)
    loss_ref[...] = jnp.zeros_like(loss_ref)

    def store(i, value):
        error = value - noise_ref[rows_of(i), :]
        weight = weight_ref[0:1, :]
        loss_ref[...] += jnp.sum(weight * error * error, 0, keepdims=True)
        grad_ref[rows_of(i), :] = (2.0 * weight * error / total).astype(narrow)

    conv_wide(s_ref, w_ref, store)
    wide_back(full_ref, w_ref, grad_ref, dw_ref, part_ref, send_ref, s_ref, t_ref)


def wide_back(full_ref, w_ref, grad_ref, dw_ref, part_ref, send_ref, s_ref, t_ref):
    shift_full(grad_ref, s_ref, HALF)
    transpose_into(load_rows(full_ref), t_ref)

    def keep(t, value):
        dw_ref[t * C : (t + 1) * C, :] = value.astype(narrow)

    kernel_grad(t_ref, s_ref, -1, keep)
    conv_tall(s_ref, w_ref, -1, put_split(part_ref, send_ref))


def normback_kernel(act, x_ref, part_ref, recv_ref, up_ref, norm_ref, dx_ref, low_ref, sums_ref, tmp_ref):
    def load(i):
        return part_ref[rows_of(i), :] + recv_ref[rows_of(i), :].astype(single)

    def store(i, value):
        value = value + up_ref[rows_of(i), :]
        dx_ref[rows_of(i), :] = value
        low_ref[rows_of(i), :] = value.astype(narrow)

    total, along = norm_backward(x_ref, load, norm_ref[0:1, :], norm_ref[1:2, :], act, tmp_ref, store)
    sums_ref[0:1, :] = along
    sums_ref[1:2, :] = total


def resback_kernel(
    gown_ref, gpeer_ref, hidden_ref, inner_ref, norm_ref, mod_ref, wout_ref, own_ref, peer_ref, win_ref,
    dout_ref, din_ref, part_ref, send_ref, sums_ref, dmod_ref,
    full_ref, s_ref, t_ref, dh_ref, tmp_ref, grad_ref,
):
    join_core(gown_ref, gpeer_ref, full_ref)
    transpose_into(load_rows(full_ref), t_ref)
    shift_full(hidden_ref, s_ref, HALF)

    def keep(t, value):
        dout_ref[t * C : (t + 1) * C, :] = value.astype(narrow)

    kernel_grad(t_ref, s_ref, 1, keep)
    shift_full(full_ref, s_ref, C)

    def put(i, value):
        dh_ref[rows_of(i), :] = value

    conv_back(s_ref, wout_ref, put)
    gain, bias, scale, shift = mid_rows(norm_ref, mod_ref)

    def store(i, value):
        grad_ref[rows_of(i), :] = value.astype(narrow)

    total, along = norm_backward(
        inner_ref, load_rows(dh_ref), gain * scale, bias * scale + shift, True, tmp_ref, store
    )
    sums_ref[0:1, :] = scale * along
    sums_ref[1:2, :] = scale * total
    dmod_ref[0:1, :] = gain * along + bias * total
    dmod_ref[1:2, :] = total
    join_core(own_ref, peer_ref, full_ref)
    wide_back(full_ref, win_ref, grad_ref, din_ref, part_ref, send_ref, s_ref, t_ref)


def attnback_kernel(
    gown_ref, gpeer_ref, qkv_ref, log_ref, out_ref, w_ref, own_ref, peer_ref,
    dw_ref, part_ref, send_ref,
    full_ref, t_ref, grad_ref, k_ref, kt_ref, dk_ref, dv_ref, dqkv_ref,
):
    join_core(gown_ref, gpeer_ref, full_ref)
    transpose_into(load_rows(full_ref), t_ref)
    for s in range(2):
        lanes = slice(s * BLOCK, (s + 1) * BLOCK)
        dw_ref[:, s * C + 3 * BLOCK : (s + 1) * C] = dot(t_ref[...], out_ref[:, lanes]).astype(narrow)

        @pl.loop(0, PIX // CHUNK)
        def _(i):
            at = rows_of(i)
            value = dot(full_ref[at, :], w_ref[:, s * C + 3 * BLOCK : (s + 1) * C])
            grad_ref[at, lanes] = value.astype(narrow)

    dqkv = [dqkv_ref.at[:, s * 3 * BLOCK : (s + 1) * 3 * BLOCK] for s in range(2)]
    attend_back(qkv_ref, log_ref, grad_ref, k_ref, kt_ref, dk_ref, dv_ref, dqkv)
    join_core(own_ref, peer_ref, full_ref)
    transpose_into(load_rows(full_ref), t_ref)
    for s in range(2):
        lanes = slice(s * 3 * BLOCK, (s + 1) * 3 * BLOCK)
        dw_ref[:, s * C : s * C + 3 * BLOCK] = dot(t_ref[...], dqkv_ref[:, lanes]).astype(narrow)
    store = put_split(part_ref, send_ref)

    @pl.loop(0, PIX // CHUNK)
    def _(i):
        at = rows_of(i)
        value = dot_t(dqkv_ref[at, 0 : 3 * BLOCK], w_ref[:, 0 : 3 * BLOCK])
        store(i, value + dot_t(dqkv_ref[at, 3 * BLOCK :], w_ref[:, C : C + 3 * BLOCK]))


HALF_F32 = struct((PIX, HALF))
HALF_LOW = struct((PIX, HALF), narrow)
FULL_LOW = pltpu.VMEM((PIX, C), narrow)
SHIFTED = pltpu.VMEM((3, ROWS, C), narrow)
TURNED = pltpu.VMEM((C, PIX), narrow)
SWAP = [(0, 1), (1, 0)]


def core_swap(value):
    return lax.ppermute(value, "lo", SWAP)


def image_swap(value):
    return lax.ppermute(value, "hi", SWAP)


DP = ("dz", "dy")


def pick_image(value):
    hi = lax.axis_index("hi")
    kept = jnp.where(hi == 0, value[0], value[1])
    came = image_swap(jnp.where(hi == 0, value[1], value[0]))
    return jnp.where(hi == 0, jnp.concatenate([kept, came], 1), jnp.concatenate([came, kept], 1))


def join_image(value, axis):
    hi = lax.axis_index("hi")
    came = image_swap(value)
    return jnp.where(
        hi == 0, jnp.concatenate([value, came], axis), jnp.concatenate([came, value], axis)
    )


def gather_weight(shard):
    rows = lax.all_gather(shard, DP, axis=0, tiled=True)
    return lax.all_gather(rows, "hi", axis=1, tiled=True)


def scatter_grad(value):
    cols = lax.psum_scatter(value, "hi", scatter_dimension=1, tiled=True)
    return lax.psum_scatter(cols, DP, scatter_dimension=0, tiled=True).astype(single)


def chan_index():
    return lax.axis_index("hi") * 2 + lax.axis_index("lo")


def sinusoid_of(timesteps):
    half_count = TF // 2
    frequency = jnp.exp(-math.log(10000.0) * jnp.arange(half_count, dtype=single) / half_count)
    angles = timesteps.astype(single)[:, None] * frequency[None, :]
    return jnp.concatenate([jnp.cos(angles), jnp.sin(angles)], 1).astype(narrow)


def embed_forward(timesteps, classes, time_in, emb_out, emb_proj):
    times = lax.all_gather(timesteps, DP, axis=0, tiled=True)
    labels = lax.all_gather(classes, DP, axis=0, tiled=True)
    rows = time_in.shape[0]
    place = lax.axis_index(DP) * rows
    sinusoid = lax.dynamic_slice_in_dim(sinusoid_of(times), place, rows, 1)
    pre = lax.psum(dot(sinusoid, time_in), DP)
    hidden = jax.nn.silu(pre).astype(narrow)
    class_here = emb_out.shape[1] - hidden.shape[1]
    numbers = chan_index() * class_here + jnp.arange(class_here)
    onehot = (labels[:, None] == numbers[None, :]).astype(narrow)
    joined = jnp.concatenate([hidden, onehot], 1)
    embedding = lax.psum(dot_t(joined, emb_out), ("hi", "lo"))
    context = jax.nn.silu(embedding).astype(narrow)
    parts = jnp.einsum("be,lej->blj", context, emb_proj, preferred_element_type=single)
    mine = lax.psum_scatter(parts, DP, scatter_dimension=0, tiled=True)
    hi = lax.axis_index("hi")
    kept = jnp.where(hi == 0, mine[0], mine[1])
    came = image_swap(jnp.where(hi == 0, mine[1], mine[0]))
    wide = jnp.where(hi == 0, jnp.concatenate([kept, came], 1), jnp.concatenate([came, kept], 1))
    modulate = jnp.swapaxes(wide.reshape(2, HALF, 2), 1, 2)
    return modulate, (sinusoid, pre, joined, embedding, context)


def embed_backward(saved, dmod, emb_proj, emb_out):
    sinusoid, pre, joined, embedding, context = saved
    flat = jnp.swapaxes(dmod, 1, 2).reshape(2, 2 * HALF).astype(narrow)
    hi = lax.axis_index("hi")
    width = flat.shape[1] // 2
    kept = jnp.where(hi == 0, flat[:, :width], flat[:, width:])
    came = image_swap(jnp.where(hi == 0, flat[:, width:], flat[:, :width]))
    both = jnp.where(hi == 0, jnp.stack([kept, came]), jnp.stack([came, kept]))
    grads = lax.all_gather(both, DP, axis=0, tiled=True)
    proj_grad = jnp.einsum("be,blj->lej", context, grads, preferred_element_type=single)
    part = jnp.einsum("blj,lej->be", grads, emb_proj, preferred_element_type=single)
    context_grad = lax.psum(part, ("hi", "lo"))
    _, pullback = jax.vjp(jax.nn.silu, embedding)
    (embed_grad,) = pullback(context_grad)
    embed_low = embed_grad.astype(narrow)
    out_grad = jnp.einsum("be,bj->ej", embed_low, joined, preferred_element_type=single)
    joined_grad = lax.psum(dot(embed_low, emb_out[:, : pre.shape[1]]), DP)
    _, pullback = jax.vjp(jax.nn.silu, pre)
    (pre_grad,) = pullback(joined_grad)
    time_grad = jnp.einsum("bt,be->te", sinusoid, pre_grad.astype(narrow), preferred_element_type=single)
    return proj_grad, time_grad, out_grad


def res_forward(own, peer, win, wout, norm, mod):
    outs = [HALF_F32, HALF_LOW, HALF_F32, HALF_LOW]
    return call(res_kernel, outs, [FULL_LOW, SHIFTED], [own, peer, win, wout, norm, mod], "res_forward")


def res_backward(gown, gpeer, hidden, inner, norm, mod, wout, own, peer, win):
    taps = struct((9 * C, HALF), narrow)
    outs = [taps, taps, HALF_F32, HALF_LOW, struct((2, HALF)), struct((2, HALF))]
    scratch = [FULL_LOW, SHIFTED, TURNED, pltpu.VMEM((PIX, HALF), single), pltpu.VMEM((PIX, HALF), single), pltpu.VMEM((PIX, HALF), narrow)]
    return call(resback_kernel, outs, scratch, [gown, gpeer, hidden, inner, norm, mod, wout, own, peer, win], "res_backward")


def norm_step(act, x, part, recv, up, norm):
    outs = [HALF_F32, HALF_LOW, struct((2, HALF))]
    body = functools.partial(normback_kernel, act)
    return call(body, outs, [pltpu.VMEM((PIX, HALF), single)], [x, part, recv, up, norm], "norm_backward")


def entry_step(act, x, part, recv, norm):
    return call(functools.partial(entry_kernel, act), [HALF_F32, HALF_LOW], [], [x, part, recv, norm], "entry")


def network(noisy, noise, sample_weight, kernels_in, kernels_out, attn, norms, modulate):
    images = noisy.shape[0] * lax.axis_size("dz") * lax.axis_size("dy")
    total = float(images * PIX * C)
    x0 = pick_image(noisy.reshape(2, PIX, BLOCK))
    target = pick_image(noise.reshape(2, PIX, BLOCK))
    weight = jnp.where(lax.axis_index("hi") == 0, sample_weight[0], sample_weight[1])
    weight = jnp.broadcast_to(weight, (8, HALF))
    stream0, entry0 = call(first_kernel, [HALF_F32, HALF_LOW], [], [x0, norms[0]], "entry")
    peer0 = core_swap(entry0)
    inner0, hidden0, part, send = res_forward(entry0, peer0, kernels_in[0], kernels_out[0], norms[1], modulate[0])
    stream1, entry1 = entry_step(False, stream0, part, core_swap(send), norms[2])
    peer1 = core_swap(entry1)
    outs = [struct((PIX, 6 * BLOCK), narrow), struct((4, PIX // CHUNK, 1, CHUNK)), HALF_LOW, HALF_F32, HALF_LOW]
    scratch = [FULL_LOW, pltpu.VMEM((PIX, BLOCK), narrow), pltpu.VMEM((BLOCK, PIX), narrow)]
    qkv, log, attended, part, send = call(attn_kernel, outs, scratch, [entry1, peer1, attn], "attention")
    stream2, entry2 = entry_step(True, stream1, part, core_swap(send), norms[3])
    peer2 = core_swap(entry2)
    inner2, hidden2, part, send = res_forward(entry2, peer2, kernels_in[1], kernels_out[1], norms[4], modulate[1])
    stream3, entry3 = entry_step(True, stream2, part, core_swap(send), norms[5])
    peer3 = core_swap(entry3)
    taps = struct((9 * C, HALF), narrow)
    outs = [struct((1, HALF)), taps, HALF_F32, HALF_LOW]
    scratch = [FULL_LOW, SHIFTED, TURNED, pltpu.VMEM((PIX, HALF), narrow)]
    args = [entry3, peer3, kernels_in[2], target, weight]
    loss, din2, part, send = call(functools.partial(head_kernel, total), outs, scratch, args, "head")
    zero = jnp.zeros((PIX, HALF), single)
    grad3, low3, sums5 = norm_step(True, stream3, part, core_swap(send), zero, norms[5])
    dout1, din1, part, send, sums4, dmod1 = res_backward(
        low3, core_swap(low3), hidden2, inner2, norms[4], modulate[1], kernels_out[1], entry2, peer2, kernels_in[1]
    )
    grad2, low2, sums3 = norm_step(True, stream2, part, core_swap(send), grad3, norms[3])
    outs = [struct((C, 2 * C), narrow), HALF_F32, HALF_LOW]
    scratch = [
        FULL_LOW, TURNED, pltpu.VMEM((PIX, HALF), narrow), pltpu.VMEM((PIX, BLOCK), narrow), pltpu.VMEM((BLOCK, PIX), narrow),
        pltpu.VMEM((PIX, BLOCK), single), pltpu.VMEM((PIX, BLOCK), single), pltpu.VMEM((PIX, 6 * BLOCK), narrow),
    ]
    args = [low2, core_swap(low2), qkv, log, attended, attn, entry1, peer1]
    dattn, part, send = call(attnback_kernel, outs, scratch, args, "attention_backward")
    grad1, low1, sums2 = norm_step(False, stream1, part, core_swap(send), grad2, norms[2])
    dout0, din0, part, send, sums1, dmod0 = res_backward(
        low1, core_swap(low1), hidden0, inner0, norms[1], modulate[0], kernels_out[0], entry0, peer0, kernels_in[0]
    )
    _, _, sums0 = norm_step(True, stream0, part, core_swap(send), grad1, norms[0])
    sums = jnp.stack([sums0, sums1, sums2, sums3, sums4, sums5])
    return jnp.sum(loss) / total, (din0, din1, din2), (dout0, dout1), dattn, sums, jnp.stack([dmod0, dmod1])


MESH = pl.DeviceIdType.MESH
ANY = pl.BlockSpec(memory_space=pl.ANY)
LAYERS = 6
STEPS = 10


def remote(src, dst, send, recv, **where):
    return pltpu.make_async_remote_copy(
        src_ref=src, dst_ref=dst, send_sem=send, recv_sem=recv, device_id=where, device_id_type=MESH
    )


def place():
    return lax.axis_index("dz"), lax.axis_index("dy"), lax.axis_index("hi")


def greet(others):
    barrier = pltpu.get_barrier_semaphore()
    for where in others:
        pl.semaphore_signal(barrier, inc=1, device_id=where, device_id_type=MESH)
    pl.semaphore_wait(barrier, len(others))


def neighbours():
    z, y, x = place()
    others = [{"dz": (z + k) % 4} for k in (1, 2, 3)]
    return others + [{"dy": 1 - y}, {"hi": 1 - x}, {"lo": 1 - lax.axis_index("lo")}]


class Layout:
    def __init__(self, rows, lanes):
        self.rows, self.lanes = rows, lanes

    def block(self, zz, yy):
        return pl.ds(pl.multiple_of((zz * 2 + yy) * self.rows, 32), self.rows)

    def cols(self, xx):
        return pl.ds(pl.multiple_of(xx * self.lanes, 128), self.lanes)


class Gather:
    def __init__(self, layer, shard, full, send, recv, local):
        z, y, x = place()
        rows, lanes = shard.shape
        at = Layout(rows, lanes)
        mine = full.at[at.block(z, y), at.cols(x)]
        self.local = pltpu.make_async_copy(shard, mine, local.at[layer])

        def copy(j, src, dst, **where):
            return remote(src, dst, send.at[layer, j], recv.at[layer, j], **where)

        self.along_z = [copy(k - 1, shard, mine, dz=(z + k) % 4) for k in (1, 2, 3)]
        self.first, self.second = [], []
        for n in range(2):
            part = full.at[at.block(n, y), at.cols(x)]
            self.first.append(copy(3 + n, part, part, dy=1 - y))
            part = full.at[at.block(2 + n, y), at.cols(x)]
            self.first.append(copy(5 + n, part, part, hi=1 - x))
        part = full.at[0 : 4 * rows, at.cols(x)]
        self.second.append(copy(7, part, part, hi=1 - x))
        for n in range(2):
            part = full.at[at.block(2 + n, y), :]
            self.second.append(copy(8 + n, part, part, dy=1 - y))

    def start(self):
        self.local.start()
        for copy in self.along_z:
            copy.start()

    def turn(self):
        self.local.wait()
        for copy in self.along_z:
            copy.wait_recv()
        for copy in self.first:
            copy.start()

    def spread(self):
        for copy in self.first:
            copy.wait_recv()
        for copy in self.second:
            copy.start()

    def ready(self):
        for copy in self.second:
            copy.wait_recv()

    def drain(self):
        for copy in self.along_z + self.first + self.second:
            copy.wait_send()


def add_rows(count, lanes, into, other):
    size = 64 if lanes > 128 else 192

    @pl.loop(0, count // size)
    def _(i):
        at = pl.ds(pl.multiple_of(i * size, 32), size)
        total = into.at[at, :][...].astype(single) + other.at[at, :][...].astype(single)
        into.at[at, :][...] = total.astype(narrow)


class Reduce:
    def __init__(self, layer, grad, bufs, out, send, recv):
        z, y, x = place()
        ra, rb, rc, rd, rz = bufs
        rows, lanes = out.shape
        at = Layout(rows, lanes)
        self.rows, self.lanes, self.out, self.grad, self.bufs = rows, lanes, out, grad, bufs
        self.at, self.here = at, (z, y, x)

        def copy(j, src, dst, **where):
            return remote(src, dst, send.at[layer, j], recv.at[layer, j], **where)

        self.first = [copy(0, grad.at[0 : 4 * rows, at.cols(1 - x)], ra, hi=1 - x)]
        self.second, self.third = [], []
        for n in range(2):
            self.first.append(copy(1 + n, grad.at[at.block(2 + n, 1 - y), :], rb.at[n], dy=1 - y))
        for n in range(2):
            part = grad.at[at.block(n, 1 - y), at.cols(x)]
            self.second.append(copy(3 + n, part, rc.at[n], dy=1 - y))
        for n in range(2):
            part = grad.at[at.block(2 + n, y), at.cols(1 - x)]
            self.second.append(copy(5 + n, part, rd.at[n], hi=1 - x))
        for k in (1, 2, 3):
            zz = (z + k) % 4
            part = grad.at[at.block(zz, y), at.cols(x)]
            self.third.append(copy(6 + k, part, rz.at[k - 1], dz=zz))

    def start(self):
        for copy in self.first:
            copy.start()

    def turn(self):
        (z, y, x), at, (ra, rb, rc, rd, rz) = self.here, self.at, self.bufs
        self.first[0].wait_recv()
        add_rows(4 * self.rows, self.lanes, self.grad.at[0 : 4 * self.rows, at.cols(x)], ra)
        for copy in self.second[:2]:
            copy.start()
        for n in range(2):
            self.first[1 + n].wait_recv()
            add_rows(self.rows, 2 * self.lanes, self.grad.at[at.block(2 + n, y), :], rb.at[n])
            self.second[2 + n].start()

    def spread(self):
        (z, y, x), at, (ra, rb, rc, rd, rz) = self.here, self.at, self.bufs
        for n in range(2):
            self.second[n].wait_recv()
            add_rows(self.rows, self.lanes, self.grad.at[at.block(n, y), at.cols(x)], rc.at[n])
        for n in range(2):
            self.second[2 + n].wait_recv()
            add_rows(self.rows, self.lanes, self.grad.at[at.block(2 + n, y), at.cols(x)], rd.at[n])
        for copy in self.third:
            copy.start()

    def finish(self):
        (z, y, x), at, (ra, rb, rc, rd, rz) = self.here, self.at, self.bufs
        for copy in self.third:
            copy.wait_recv()
        size = 64
        mine = self.grad.at[at.block(z, y), at.cols(x)]

        @pl.loop(0, self.rows // size)
        def _(i):
            part = pl.ds(pl.multiple_of(i * size, 32), size)
            total = mine.at[part, :][...].astype(single)
            for k in range(3):
                total = total + rz.at[k, part, :][...].astype(single)
            self.out.at[part, :][...] = total

    def drain(self):
        for copy in self.first + self.second + self.third:
            copy.wait_send()


class Core:
    def __init__(self, send, recv):
        self.send, self.recv, self.used = send, recv, 0
        self.core = lax.axis_index("lo")

    def take(self, count):
        base = self.used
        self.used += count
        return base

    def copy(self, index, src, dst):
        return remote(src, dst, self.send.at[index], self.recv.at[index], lo=1 - self.core)

    def lanes(self, j):
        return pl.ds(pl.multiple_of((2 * j + self.core) * BLOCK, 128), BLOCK)

    def share(self, full):
        base = self.take(2 * (PIX // CHUNK))

        def copies(i):
            parts = [full.at[rows_of(i), self.lanes(j)] for j in range(2)]
            return [self.copy(base + 2 * i + j, part, part) for j, part in enumerate(parts)]

        def store(i, value):
            for j in range(2):
                full[rows_of(i), self.lanes(j)] = value[:, j * BLOCK : (j + 1) * BLOCK]
            for copy in copies(i):
                copy.start()

        def wait():
            @pl.loop(0, PIX // CHUNK)
            def _(i):
                for copy in copies(i):
                    copy.wait()

        return store, wait

    def combine(self, part, send, recv):
        base = self.take(PIX // CHUNK)

        def one(i):
            return self.copy(base + i, send.at[rows_of(i), :], recv.at[rows_of(i), :])

        def store(i, value):
            own, peer = split_core(value)
            part[rows_of(i), :] = own
            send[rows_of(i), :] = peer.astype(narrow)
            one(i).start()

        def wait():
            @pl.loop(0, PIX // CHUNK)
            def _(i):
                one(i).wait()

        def load(i):
            return part[rows_of(i), :] + recv[rows_of(i), :].astype(single)

        return store, wait, load


class Spill:
    def __init__(self, sems):
        self.sems, self.used, self.open = sems, 0, []

    def start(self, src, dst):
        copy = pltpu.make_async_copy(src, dst, self.sems.at[self.used])
        self.used += 1
        copy.start()
        self.open.append(copy)
        return copy

    def finish(self, copy):
        copy.wait()
        self.open = [other for other in self.open if other is not copy]

    def drain(self):
        for copy in self.open:
            copy.wait()


def forward_kernel(
    total,
    x0_ref, noise_hbm, weight_ref, norms_ref, mod_ref, s0, s1, s2, s3, s4, s5,
    w0_out, w1_out, w2_out, w3_out, w4_out, w5_out,
    full0_out, full1_out, full2_out, full3_out, x1_out, x2_out, x3_out,
    inner0_out, inner2_out, hidden0_out, hidden2_out, qkv_out, att_out, pg_out, log_ref, loss_ref,
    w0, w1, w2, w3, w4, w5,
    full0, full1, full2, full3, x1, x2, x3, inner0, inner2, hidden0, hidden2, qkv, att, pg, noise_ref,
    shifted, part, send0, send1, send2, recv0, recv1, recv2, k_ref, vt_ref,
    gsend, grecv, glocal, csend, crecv, lsem,
):
    greet(neighbours())
    gathers = [
        Gather(n, shard, full, gsend, grecv, glocal)
        for n, (shard, full) in enumerate(zip((s0, s1, s2, s3, s4, s5), (w0, w1, w2, w3, w4, w5)))
    ]
    for gather in gathers:
        gather.start()
    spill, core = Spill(lsem), Core(csend, crecv)
    noise_here = spill.start(noise_hbm, noise_ref)

    def norm_row(n):
        return norms_ref[n, 0:1, :], norms_ref[n, 1:2, :]

    class First:
        def __getitem__(self, at):
            return x0_ref[at].astype(single)

    def entry(x, n, act, full):
        gain, bias = norm_row(n)
        store, wait = core.share(full)
        norm_forward(x, gain, bias, act, store)
        return wait

    def residual(full, w_in, w_out, ready, n, layer, inner, hidden, send, recv):
        shift_full(full, shifted, C)

        def put(i, value):
            inner[rows_of(i), :] = value

        conv_wide(shifted, w_in, put)
        gain, bias = norm_row(n)
        scale, shift = 1.0 + mod_ref[layer, 0:1, :], mod_ref[layer, 1:2, :]

        def keep(i, value):
            hidden[rows_of(i), :] = value

        norm_forward(inner, gain * scale, bias * scale + shift, True, keep)
        shift_full(hidden, shifted, HALF)
        ready()
        store, wait, load = core.combine(part, send, recv)
        conv_tall(shifted, w_out, 1, store)
        return wait, load

    def advance(x_old, load, x_new):
        @pl.loop(0, PIX // CHUNK)
        def _(i):
            x_new[rows_of(i), :] = x_old[rows_of(i), :] + load(i)

    def after(n, copies):
        gathers[n].ready()
        spill.start(copies[0], copies[1])

    wait = entry(First(), 0, True, full0)
    gathers[0].turn()
    gathers[1].turn()
    gathers[0].spread()
    gathers[2].turn()
    gathers[1].spread()
    wait()
    spill.start(full0, full0_out)
    after(0, (w0, w0_out))

    def ready1():
        gathers[3].turn()
        gathers[2].spread()
        after(1, (w1, w1_out))

    wait, load = residual(full0, w0, w1, ready1, 1, 0, inner0, hidden0, send0, recv0)
    spill.start(inner0, inner0_out)
    spill.start(hidden0, hidden0_out)
    wait()
    advance(First(), load, x1)
    spill.start(x1, x1_out)
    wait = entry(x1, 2, False, full1)
    gathers[4].turn()
    gathers[3].spread()
    after(2, (w2, w2_out))
    wait()
    spill.start(full1, full1_out)

    @pl.loop(0, PIX // CHUNK)
    def _(i):
        at = rows_of(i)
        for s in range(2):
            value = dot(full1[at, :], w2[:, s * C : s * C + 3 * BLOCK])
            qkv[at, s * 3 * BLOCK : (s + 1) * 3 * BLOCK] = value.astype(narrow)

    spill.start(qkv, qkv_out)
    attend(qkv, k_ref, vt_ref, log_ref, att)
    spill.start(att, att_out)
    gathers[5].turn()
    gathers[4].spread()
    store, wait, load = core.combine(part, send1, recv1)

    @pl.loop(0, PIX // CHUNK)
    def _(i):
        at = rows_of(i)
        value = dot_t(att[at, 0:BLOCK], w2[:, 3 * BLOCK : C])
        store(i, value + dot_t(att[at, BLOCK:], w2[:, C + 3 * BLOCK :]))

    wait()
    advance(x1, load, x2)
    spill.start(x2, x2_out)
    wait = entry(x2, 3, True, full2)
    after(3, (w3, w3_out))
    wait()
    spill.start(full2, full2_out)

    def ready4():
        gathers[5].spread()
        after(4, (w4, w4_out))

    wait, load = residual(full2, w3, w4, ready4, 4, 1, inner2, hidden2, send2, recv2)
    spill.start(inner2, inner2_out)
    spill.start(hidden2, hidden2_out)
    wait()
    advance(x2, load, x3)
    spill.start(x3, x3_out)
    wait = entry(x3, 5, True, full3)
    after(5, (w5, w5_out))
    wait()
    spill.start(full3, full3_out)
    shift_full(full3, shifted, C)
    spill.finish(noise_here)
    loss_ref[...] = jnp.zeros_like(loss_ref)

    def store(i, value):
        error = value - noise_ref[rows_of(i), :]
        weight = weight_ref[0:1, :]
        loss_ref[...] += jnp.sum(weight * error * error, 0, keepdims=True)
        pg[rows_of(i), :] = (2.0 * weight * error / total).astype(narrow)

    conv_wide(shifted, w5, store)
    spill.start(pg, pg_out)
    for gather in gathers:
        gather.drain()
    spill.drain()


def backward_kernel(
    norms_ref, mod_ref, log_ref,
    x0_hbm, w0_hbm, w1_hbm, w2_hbm, w3_hbm, w4_hbm, w5_hbm,
    full0_hbm, full1_hbm, full2_hbm, full3_hbm, x1_hbm, x2_hbm, x3_hbm,
    inner0_hbm, inner2_hbm, hidden0_hbm, hidden2_hbm, qkv_hbm, att_hbm, pg_hbm,
    g0, g1, g2, g3, g4, g5, sums_ref, dmod_ref,
    wa, wb, wattn, d0, d1, d2, d3, d4, d5,
    ra, rb, rc, rd, rz, qa, qb, qc, qd, qz,
    gfull3, gfull2, gfull1, entry, x_ref, x0_ref, inner, hidden, qkv, att, pg,
    shifted, turned, tmp, dh, part, up, send, recv0, recv1, recv2, recv3,
    k_ref, kt_ref, dk_ref, dv_ref,
    rsend, rrecv, csend, crecv, lsem,
):
    spill, core = Spill(lsem), Core(csend, crecv)
    load_w5 = spill.start(w5_hbm, wa)
    load_w4 = spill.start(w4_hbm, wb)
    load_pg = spill.start(pg_hbm, pg)
    load_entry = spill.start(full3_hbm, entry)
    load_x = spill.start(x3_hbm, x_ref)
    load_hidden = spill.start(hidden2_hbm, hidden)
    load_inner = spill.start(inner2_hbm, inner)
    load_qkv = spill.start(qkv_hbm, qkv)
    load_att = spill.start(att_hbm, att)
    load_attn = spill.start(w2_hbm, wattn)
    load_x0 = spill.start(x0_hbm, x0_ref)
    greet(neighbours())
    grads = [d0, d1, d2, d3, d4, d5]
    outs = [g0, g1, g2, g3, g4, g5]
    slots = {0: 0, 1: 1, 3: 2, 4: 3, 5: 4}
    reduces = []
    for n in range(LAYERS):
        bufs = (qa, qb, qc, qd, qz) if n == 2 else tuple(buf.at[slots[n]] for buf in (ra, rb, rc, rd, rz))
        reduces.append(Reduce(n, grads[n], bufs, outs[n], rsend, rrecv))

    def norm_row(n):
        return norms_ref[n, 0:1, :], norms_ref[n, 1:2, :]

    def keep_taps(grad):
        def keep(t, value):
            grad[t * C : (t + 1) * C, :] = value.astype(narrow)

        return keep

    def wide(w, grad, n, recv):
        shift_full(pg, shifted, HALF)
        transpose_into(load_rows(entry), turned)
        kernel_grad(turned, shifted, -1, keep_taps(grad))
        reduces[n].start()
        store, wait, load = core.combine(part, send, recv)
        conv_tall(shifted, w, -1, store)
        return wait, load

    def through_norm(x, load, n, act, first, gfull):
        gain, bias = norm_row(n)
        if gfull is not None:
            share, wait = core.share(gfull)
        else:
            share, wait = None, None

        def store(i, value):
            if share is None:
                return
            if not first:
                value = value + up[rows_of(i), :]
            up[rows_of(i), :] = value
            share(i, value.astype(narrow))

        summed, along = norm_backward(x, load, gain, bias, act, tmp, store)
        sums_ref[n, 0:1, :] = along
        sums_ref[n, 1:2, :] = summed
        return wait

    def residual(gfull, w_out, n_out, n_norm, layer):
        transpose_into(load_rows(gfull), turned)
        shift_full(hidden, shifted, HALF)
        kernel_grad(turned, shifted, 1, keep_taps(grads[n_out]))
        reduces[n_out].start()
        shift_full(gfull, shifted, C)

        def put(i, value):
            dh[rows_of(i), :] = value

        conv_back(shifted, w_out, put)
        gain, bias = norm_row(n_norm)
        scale, shift = 1.0 + mod_ref[layer, 0:1, :], mod_ref[layer, 1:2, :]

        def store(i, value):
            pg[rows_of(i), :] = value.astype(narrow)

        summed, along = norm_backward(inner, load_rows(dh), gain * scale, bias * scale + shift, True, tmp, store)
        sums_ref[n_norm, 0:1, :] = scale * along
        sums_ref[n_norm, 1:2, :] = scale * summed
        dmod_ref[layer, 0:1, :] = gain * along + bias * summed
        dmod_ref[layer, 1:2, :] = summed

    done = spill.finish
    done(load_pg)
    done(load_entry)
    done(load_w5)
    wait, load = wide(wa, d5, 5, recv0)
    load_w3 = spill.start(w3_hbm, wa)
    load_entry = spill.start(full2_hbm, entry)
    done(load_x)
    wait()
    wait = through_norm(x_ref, load, 5, True, True, gfull3)
    load_x = spill.start(x2_hbm, x_ref)
    reduces[5].turn()
    wait()
    done(load_hidden)
    done(load_inner)
    done(load_w4)
    residual(gfull3, wb, 4, 4, 1)
    load_hidden = spill.start(hidden0_hbm, hidden)
    load_inner = spill.start(inner0_hbm, inner)
    load_w1 = spill.start(w1_hbm, wb)
    reduces[5].spread()
    done(load_entry)
    done(load_w3)
    wait, load = wide(wa, d3, 3, recv1)
    load_w0 = spill.start(w0_hbm, wa)
    load_entry = spill.start(full1_hbm, entry)
    reduces[4].turn()
    done(load_x)
    wait()
    wait = through_norm(x_ref, load, 3, True, False, gfull2)
    load_x = spill.start(x1_hbm, x_ref)
    reduces[3].turn()
    reduces[4].spread()
    reduces[5].finish()
    wait()
    done(load_qkv)
    done(load_att)
    done(load_attn)
    transpose_into(load_rows(gfull2), turned)
    for s in range(2):
        lanes = slice(s * BLOCK, (s + 1) * BLOCK)
        d2[:, s * C + 3 * BLOCK : (s + 1) * C] = dot(turned[...], att[:, lanes]).astype(narrow)

        @pl.loop(0, PIX // CHUNK)
        def _(i):
            at = rows_of(i)
            value = dot(gfull2[at, :], wattn[:, s * C + 3 * BLOCK : (s + 1) * C])
            pg[at, lanes] = value.astype(narrow)

    dqkv = [shifted.at[s, 0:PIX, 0 : 3 * BLOCK] for s in range(2)]
    attend_back(qkv, log_ref, pg, k_ref, kt_ref, dk_ref, dv_ref, dqkv)
    done(load_entry)
    transpose_into(load_rows(entry), turned)
    for s in range(2):
        d2[:, s * C : s * C + 3 * BLOCK] = dot(turned[...], dqkv[s][...]).astype(narrow)
    reduces[2].start()
    store, wait, load = core.combine(part, send, recv2)

    @pl.loop(0, PIX // CHUNK)
    def _(i):
        at = rows_of(i)
        value = dot_t(dqkv[0].at[at, :][...], wattn[:, 0 : 3 * BLOCK])
        store(i, value + dot_t(dqkv[1].at[at, :][...], wattn[:, C : C + 3 * BLOCK]))

    load_entry = spill.start(full0_hbm, entry)
    done(load_x)
    wait()
    wait = through_norm(x_ref, load, 2, False, False, gfull1)
    reduces[3].spread()
    reduces[2].turn()
    reduces[4].finish()
    wait()
    done(load_hidden)
    done(load_inner)
    done(load_w1)
    residual(gfull1, wb, 1, 1, 0)
    reduces[2].spread()
    reduces[3].finish()
    done(load_entry)
    done(load_w0)
    wait, load = wide(wa, d0, 0, recv3)
    reduces[1].turn()
    reduces[2].finish()
    wait()
    done(load_x0)

    class First:
        def __getitem__(self, at):
            return x0_ref[at].astype(single)

    through_norm(First(), load, 0, True, False, None)
    reduces[0].turn()
    reduces[1].spread()
    reduces[0].spread()
    reduces[1].finish()
    reduces[0].finish()
    for reduce in reduces:
        reduce.drain()
    spill.drain()


def vmem(shape, dtype=single):
    return pltpu.VMEM(shape, dtype)


def semaphores(*shape):
    return pltpu.SemaphoreType.DMA(shape)


TAPS_SHAPE = (9 * C, HALF)
ATTN_SHAPE = (C, 2 * C)
FULL = (PIX, C)
OWN = (PIX, HALF)
QKV = (PIX, 6 * BLOCK)
LOGS = (4, PIX // CHUNK, 1, CHUNK)
WEIGHTS = [TAPS_SHAPE, TAPS_SHAPE, ATTN_SHAPE, TAPS_SHAPE, TAPS_SHAPE, TAPS_SHAPE]


def fused(body, outs, out_specs, in_specs, scratch, args, number, limit, name):
    return pl.pallas_call(
        body,
        out_shape=outs,
        in_specs=in_specs,
        out_specs=out_specs,
        scratch_shapes=scratch,
        compiler_params=pltpu.CompilerParams(
            vmem_limit_bytes=limit * 2**20, collective_id=number, has_side_effects=True
        ),
        name=name,
    )(*args)


def fused_network(noisy, noise, sample_weight, shards, norms, modulate):
    images = noisy.shape[0] * lax.axis_size("dz") * lax.axis_size("dy")
    total = float(images * PIX * C)
    x0 = pick_image(noisy.reshape(2, PIX, BLOCK))
    target = pick_image(noise.reshape(2, PIX, BLOCK))
    weight = jnp.where(lax.axis_index("hi") == 0, sample_weight[0], sample_weight[1])
    weight = jnp.broadcast_to(weight, (8, HALF))
    low_shapes = WEIGHTS + [FULL] * 4
    kept = [struct(s, narrow) for s in low_shapes] + [struct(OWN)] * 5
    kept += [struct(OWN, narrow)] * 2 + [struct(QKV, narrow)] + [struct(OWN, narrow)] * 2
    outs = kept + [struct(LOGS), struct((1, HALF))]
    scratch = [vmem(s, narrow) for s in low_shapes] + [vmem(OWN)] * 5
    scratch += [vmem(OWN, narrow)] * 2 + [vmem(QKV, narrow)] + [vmem(OWN, narrow)] * 2 + [vmem(OWN)]
    scratch += [vmem((3, ROWS, C), narrow), vmem(OWN)] + [vmem(OWN, narrow)] * 6
    scratch += [vmem((PIX, BLOCK), narrow), vmem((BLOCK, PIX), narrow)]
    scratch += [semaphores(LAYERS, STEPS)] * 2 + [semaphores(LAYERS), semaphores(48), semaphores(48), semaphores(32)]
    args = [x0, target, weight, norms, modulate, *shards]
    in_specs = [VMEM, ANY, VMEM, VMEM, VMEM] + [ANY] * 6
    body = functools.partial(forward_kernel, total)
    out_specs = [ANY] * len(kept) + [VMEM] * 2
    results = fused(body, outs, out_specs, in_specs, scratch, args, 1, 56, "forward")
    w0, w1, w2, w3, w4, w5, *acts, log, loss = results
    outs = [struct(shard.shape) for shard in shards] + [struct((6, 2, HALF)), struct((2, 2, HALF))]
    scratch = [vmem(TAPS_SHAPE, narrow)] * 2 + [vmem(ATTN_SHAPE, narrow)] + [vmem(s, narrow) for s in WEIGHTS]
    for lead, (rows, lanes) in ((5, shards[0].shape), (None, shards[2].shape)):
        shapes = [(4 * rows, lanes), (2, rows, 2 * lanes), (2, rows, lanes), (2, rows, lanes), (3, rows, lanes)]
        scratch += [vmem(s if lead is None else (lead, *s), narrow) for s in shapes]
    scratch += [vmem(FULL, narrow)] * 4 + [vmem(OWN), vmem(OWN, narrow), vmem(OWN), vmem(OWN, narrow)]
    scratch += [vmem(QKV, narrow), vmem(OWN, narrow), vmem(OWN, narrow)]
    scratch += [vmem((3, ROWS, C), narrow), vmem((C, PIX), narrow)] + [vmem(OWN)] * 4 + [vmem(OWN, narrow)] * 5
    scratch += [vmem((PIX, BLOCK), narrow), vmem((BLOCK, PIX), narrow)] + [vmem((PIX, BLOCK))] * 2
    scratch += [semaphores(LAYERS, STEPS)] * 2 + [semaphores(48), semaphores(48), semaphores(32)]
    args = [norms, modulate, log, x0, w0, w1, w2, w3, w4, w5, *acts]
    in_specs = [VMEM] * 3 + [ANY] * (len(args) - 3)
    *grads, sums, dmod = fused(
        backward_kernel, outs, [VMEM] * len(outs), in_specs, scratch, args, 2, 62, "backward"
    )
    return jnp.sum(loss) / total, grads, sums, dmod


def pack_flat(members):
    return jnp.concatenate([member.reshape(-1) for member in members])


def unpack_flat(vector, shape_list):
    pieces = []
    offset = 0
    for array_shape in shape_list:
        extent = math.prod(array_shape)
        pieces.append(vector[offset : offset + extent].reshape(array_shape))
        offset += extent
    return pieces


def per_device(
    noisy,
    noise,
    timesteps,
    classes,
    sample_weight,
    conv_in,
    conv_out,
    emb_proj,
    attn_weight,
    time_in,
    emb_out,
    norms,
    conv_in_rows,
    conv_in_cols,
    conv_out_rows,
    conv_out_cols,
    emb_proj_rows,
    emb_proj_cols,
    attn_rows,
    attn_cols,
    time_rows,
    time_cols,
    embout_rows,
    embout_cols,
    norm_second,
):
    masters = [conv_in, conv_out, emb_proj, attn_weight[None], time_in[None], emb_out[None]]
    lowered = [master.astype(narrow) for master in masters]
    modulate, saved = embed_forward(timesteps, classes, lowered[4][0], lowered[5][0], lowered[2])
    norms_wide = join_image(norms, 2)
    shards = [lowered[0][0], lowered[1][0], lowered[3][0], lowered[0][1], lowered[1][1], lowered[0][2]]
    if lax.axis_size("dz") == 4 and shards[0].shape[0] % 64 == 0 and shards[2].shape[0] % 64 == 0:
        loss_part, reduced_parts, sums, dmod = fused_network(
            noisy, noise, sample_weight, shards, norms_wide, modulate
        )
    else:
        full = [gather_weight(shard) for shard in shards]
        loss_part, din, dout, dattn, sums, dmod = network(
            noisy, noise, sample_weight, (full[0], full[3], full[5]), (full[1], full[4]), full[2], norms_wide, modulate
        )
        reduced_parts = [scatter_grad(part) for part in (din[0], dout[0], dattn, din[1], dout[1], din[2])]
    in0_grad, out0_grad, attn_grad, in1_grad, out1_grad, head_grad = reduced_parts
    proj_grad, time_grad, embout_grad = embed_backward(saved, dmod, lowered[2], lowered[5][0])
    norm_local = lax.psum_scatter(sums, "hi", scatter_dimension=2, tiled=True)
    reduced = [
        jnp.stack([in0_grad, in1_grad, head_grad]),
        jnp.stack([out0_grad, out1_grad]),
        proj_grad,
        attn_grad[None],
        time_grad[None],
        embout_grad[None],
    ]
    decay_rate = 1.0 - STEP ** (-0.8)
    dp_count = lax.axis_size("dz") * lax.axis_size("dy")
    chan_count = lax.axis_size("hi") * lax.axis_size("lo")
    rows_old = [
        conv_in_rows,
        conv_out_rows,
        emb_proj_rows,
        attn_rows[None],
        time_rows[None],
        embout_rows[None],
    ]
    cols_old = [
        conv_in_cols,
        conv_out_cols,
        emb_proj_cols,
        attn_cols[None],
        time_cols[None],
        embout_cols[None],
    ]
    squares = [gradient * gradient + tiny_square for gradient in reduced]
    full_rows = [squared.shape[1] * dp_count for squared in squares]
    full_cols = [squared.shape[2] * chan_count for squared in squares]
    row_parts = [jnp.sum(squared, 2) for squared in squares]
    col_parts = [jnp.sum(squared, 1) for squared in squares]
    row_shapes = [member.shape for member in row_parts]
    col_shapes = [member.shape for member in col_parts]
    norm_width = norm_local.shape[2]
    row_totals = unpack_flat(lax.psum(pack_flat(row_parts), ("hi", "lo")), row_shapes)
    rows_new = [
        decay_rate * rows_old[position]
        + (1.0 - decay_rate) * row_totals[position] / full_cols[position]
        for position in range(6)
    ]
    row_sums_local = [jnp.sum(member, 1) for member in rows_new]
    col_vector, norm_total = lax.psum((pack_flat(col_parts + row_sums_local), norm_local), DP)
    col_pieces = unpack_flat(col_vector, col_shapes + [(member.shape[0],) for member in rows_new])
    col_totals = col_pieces[:6]
    row_means = [col_pieces[6 + position] / full_rows[position] for position in range(6)]
    cols_new = [
        decay_rate * cols_old[position]
        + (1.0 - decay_rate) * col_totals[position] / full_rows[position]
        for position in range(6)
    ]
    updates = [
        reduced[position]
        * lax.rsqrt(rows_new[position] / row_means[position][:, None])[:, :, None]
        * lax.rsqrt(cols_new[position])[:, None, :]
        for position in range(6)
    ]
    second_new = decay_rate * norm_second + (1.0 - decay_rate) * (
        norm_total * norm_total + tiny_square
    )
    norm_update = norm_total * lax.rsqrt(second_new)
    update_squares = pack_flat([jnp.sum(member * member, (1, 2)) for member in updates])
    weight_squares = pack_flat([jnp.sum(master * master, (1, 2)) for master in masters])
    norm_update_sq = jnp.sum(norm_update * norm_update, 2) / dp_count
    norm_weight_sq = jnp.sum(norms * norms, 2) / dp_count
    update_total, weight_total, norm_update_total, norm_weight_total, loss = lax.psum(
        (update_squares, weight_squares, norm_update_sq, norm_weight_sq, loss_part), ("dz", "dy", "hi", "lo")
    )
    layer_shapes = [(member.shape[0],) for member in masters]
    update_sums = unpack_flat(update_total, layer_shapes)
    weight_sums = unpack_flat(weight_total, layer_shapes)
    results = [loss]
    for position in range(6):
        entries = float(full_rows[position] * full_cols[position])
        clip_factor = jnp.maximum(1.0, jnp.sqrt(update_sums[position] / entries))
        scale_factor = jnp.maximum(floor_scale, jnp.sqrt(weight_sums[position] / entries))
        weight_new = (
            masters[position]
            - (step_rate * scale_factor / clip_factor)[:, None, None] * updates[position]
        )
        if position >= 3:
            results += [
                reduced[position][0],
                rows_new[position][0],
                cols_new[position][0],
                weight_new[0],
            ]
        else:
            results += [reduced[position], rows_new[position], cols_new[position], weight_new]
    norm_entries = float(norm_width * chan_count)
    norm_clip = jnp.maximum(1.0, jnp.sqrt(norm_update_total / norm_entries))
    norm_scale = jnp.maximum(floor_scale, jnp.sqrt(norm_weight_total / norm_entries))
    norms_new = norms - (step_rate * norm_scale / norm_clip)[:, :, None] * norm_update
    results += [norm_total, second_new, norms_new]
    return (
        results[0],
        results[1],
        results[2],
        results[3],
        results[4],
        results[5],
        results[6],
        results[7],
        results[8],
        results[9],
        results[10],
        results[11],
        results[12],
        results[13],
        results[14],
        results[15],
        results[16],
        results[17],
        results[18],
        results[19],
        results[20],
        results[21],
        results[22],
        results[23],
        results[24],
        results[25],
        results[26],
        results[27],
    )


CHAN = ("hi", "lo")


def solution(mesh):
    dp, chan = mesh.shape["dp"], mesh.shape["chan"]
    mesh = Mesh(mesh.devices.reshape(dp // 2, 2, 2, chan // 2), DP + CHAN)
    in_specs = (
        P(DP, None, None, CHAN),
        P(DP, None, None, CHAN),
        P(DP),
        P(DP),
        P(DP),
        P(None, DP, CHAN),
        P(None, DP, CHAN),
        P(None, DP, CHAN),
        P(DP, CHAN),
        P(DP, CHAN),
        P(DP, CHAN),
        P(None, None, CHAN),
        P(None, DP),
        P(None, CHAN),
        P(None, DP),
        P(None, CHAN),
        P(None, DP),
        P(None, CHAN),
        P(DP),
        P(CHAN),
        P(DP),
        P(CHAN),
        P(DP),
        P(CHAN),
        P(None, None, CHAN),
    )
    out_specs = (
        P(),
        P(None, DP, CHAN),
        P(None, DP),
        P(None, CHAN),
        P(None, DP, CHAN),
        P(None, DP, CHAN),
        P(None, DP),
        P(None, CHAN),
        P(None, DP, CHAN),
        P(None, DP, CHAN),
        P(None, DP),
        P(None, CHAN),
        P(None, DP, CHAN),
        P(DP, CHAN),
        P(DP),
        P(CHAN),
        P(DP, CHAN),
        P(DP, CHAN),
        P(DP),
        P(CHAN),
        P(DP, CHAN),
        P(DP, CHAN),
        P(DP),
        P(CHAN),
        P(DP, CHAN),
        P(None, None, CHAN),
        P(None, None, CHAN),
        P(None, None, CHAN),
    )
    return jax.shard_map(
        per_device, mesh=mesh, in_specs=in_specs, out_specs=out_specs, check_vma=False
    )
```

time: 1810 us -> 658 us (0.36)
  waiting for transfers between devices: 755 us -> 0.03 us
  matrix products: 457 us -> 5.77 us
  Pallas kernels: 0 us -> 306 us
  local copies, waits for them, and re-layouts: 283 us -> 26.7 us
  other arithmetic: 92.7 us -> 47.8 us
  blocking collectives: 191 us -> 232 us
    dot_general x165 -> x6, matrix products: 444 us -> 4.37 us  [the longest x2 1.97 us: dot(): return jnp.dot(a, b, preferred_element_type=single)]
    reduce_scatter x5 -> x0, waiting for transfers between devices: 351 us -> none  [the longest x1 131 us: per_device(): lax.psum_scatter(local_grads[0], 'dp', scatter_dimension=1, tiled=True)]
    pallas_call x0 -> x2, Pallas kernels: none -> 306 us  [fused(): pl.pallas_call(body, out_shape=outs, in_specs=in_specs, out_specs=out_spe...]
    unnamed x31 -> x2, waiting for transfers between devices: 223 us -> 0.02 us
    unnamed x349 -> x119, local copies, waits for them, and re-layouts: 230 us -> 10.3 us
    all_gather x10 -> x0, waiting for transfers between devices: 181 us -> none  [the longest x1 49.8 us: per_device(): lax.all_gather(lowered[0], 'dp', axis=1, tiled=True)]
    all_gather x3 -> x1, blocking collectives: 91.8 us -> 25.9 us  [embed_backward(): grads = lax.all_gather(both, DP, axis=0, tiled=True)]
    psum x4 -> x6, blocking collectives: 52.6 us -> 117 us  [the longest x1 34.4 us: per_device(): lax.psum((pack_flat(col_parts + row_sums_local), norm_local), DP)]
  transfers between devices with their start and end apart: 23 -> 6, of which waited for: 18 -> 0; matrix products, arithmetic and copies ran while one was open for 11% -> 6% of each run, Pallas kernels for 0% -> 0%
where the time goes in v1:
time: 658 us; the launch traced here: 647 us
  Pallas kernels  306 us (47%)
  blocking collectives  232 us (35%)
  other arithmetic  47.8 us (7%)
  local copies, waits for them, and re-layouts  26.7 us (4%)
  between operations  24.3 us (4%)
    pallas_call x2, Pallas kernels, fused(): pl.pallas_call(body, out_shape=outs, in_specs=in_specs, out_specs=out_spe...  306 us
    unnamed x2, blocking collectives  44.9 us
    psum x1, blocking collectives, per_device(): lax.psum((update_squares, weight_squares, norm_update_sq, norm_weight_sq,...  44 us
    psum x1, blocking collectives, per_device(): lax.psum((pack_flat(col_parts + row_sums_local), norm_local), DP)  34.4 us
    psum x1, blocking collectives, embed_backward(): joined_grad = lax.psum(dot(embed_low, emb_out[:, :pre.shape[1]]), DP)  31.3 us
    psum x1, blocking collectives, embed_forward(): pre = lax.psum(dot(sinusoid, time_in), DP)  29.9 us
    all_gather x1, blocking collectives, embed_backward(): grads = lax.all_gather(both, DP, axis=0, tiled=True)  25.9 us
  transfers between devices with their start and end apart: 6, of which 0 were waited for; matrix products, arithmetic and copies ran while one was open for 6% of the time, Pallas kernels for 0%

profile of v1, /device:TPU:12, one launch (start us, length us, event | category | flops | bytes accessed | tf_op | source)
XLA Modules:
  0.0 647.1 jit_solution(3869885561566685343)
XLA Ops:
  7.3 1.4 fusion.80
  9.4 0.9 dynamic-update-slice
  10.3 0.8 dynamic-update-slice.1
  11.1 10.5 %all-reduce.3 = (s32[16]{0:T(128)S(1)}, s32[16]{0:T(128)S(1)}) all-reduce(s32[16]{0:T(128)S(1)} %dynamic-update-slice.1, s32[16]{0:T(128)S(1)} %dynamic-update-slice), channel_id=1, replica_groups=mesh['dz'=4,'dy'=2,'hi'=2,'lo'=2] {'dz','dy'}, use_global_device_ids=true, to_apply=%add.1 | all-reduce | flops 32 | bytes 256
  22.3 1.0 fusion.20
  23.3 29.9 %psum.84 = f32[16,256]{1,0:T(8,128)S(1)} all-reduce(f32[16,256]{1,0:T(8,128)S(1)} %fusion.20), channel_id=1, replica_groups=mesh['dz'=4,'dy'=2,'hi'=2,'lo'=2] {'dz','dy'}, use_global_device_ids=true, to_apply=%region_0.0 | all-reduce | flops 4096 | bytes 32768 | tf_op jit(solution)/shard_map/psum | solution.py:581
  53.2 1.7 multiply_reduce_fusion.6
  55.1 5.8 psum.85
  60.9 1.1 fusion.13
  62.0 34.4 %all-reduce.2 = f32[16,2,256]{2,0,1:T(8,128)S(1)} all-reduce(f32[16,2,256]{2,0,1:T(8,128)S(1)} %fusion.13), channel_id=2, replica_groups=mesh['dz'=4,'dy'=2,'hi'=2,'lo'=2] {'dz','dy'}, use_global_device_ids=true, to_apply=%region_2.3.clone | all-reduce | flops 8192 | bytes 65536
  97.1 1.8 collective-permute-start.3
  98.8 1.9 broadcast_select_fusion.1
  101.0 0.9 slice_select_fusion.1
  101.9 1.7 collective-permute-start.1
  104.6 1.2 multiply_reduce_fusion.9
  106.4 0.9 slice_bitcast_fusion
  108.4 0.8 copy.75
  110.8 2.6 concatenate.60
  114.8 2.0 maximum_select_fusion.1.x0_ref.x0_hbm
  116.8 1.0 maximum_select_fusion.noise_hbm
  118.4 146.0 %forward.1 = (bf16[4608,256]{1,0:T(8,128)(2,1)}, bf16[4608,256]{1,0:T(8,128)(2,1)}, bf16[512,1024]{1,0:T(8,128)(2,1)}, bf16[4608,256]{1,0:T(8,128)(2,1)}, bf16[4...) custom-call(bf16[1024,256]{1,0:T(8,128)(2,1)} %maximum_select_fusion, ...), custom_call_target="tpu_custom_call" | custom-call | tf_op jit(solution)/shard_map/forward/pallas_call | solution.py:1309
  264.5 159.8 %backward.1 = (f32[576,128]{1,0:T(8,128)}, f32[576,128]{1,0:T(8,128)}, f32[64,512]{1,0:T(8,128)}, f32[576,128]{1,0:T(8,128)}, f32[576,128]{1,0:T(8,128)}, /*inde...) custom-call(f32[6,2,256]{2,1,0:T(2,128)} %maximum_select_fusion.2.norms_ref, ...), custom_call_target="tpu_custom_call" | custom-call | tf_op jit(solution)/shard_map/backward/pallas_call | solution.py:1309
  424.3 0.7 convert_bitcast_fusion
  426.4 1.9 fusion.2
  428.3 2.3 fusion
  430.6 0.7 fusion.8
  432.7 1.1 copy.80
  433.8 0.9 reshape.314
  434.8 1.3 reduce_sum.315
  436.8 0.8 broadcast_select_fusion.2
  437.5 25.9 %all_gather.11 = bf16[16,2,256]{2,1,0:T(2,128)(2,1)S(1)} all-gather(bf16[2,2,256]{2,1,0:T(2,128)(2,1)S(1)} %broadcast_select_fusion.2), channel_id=1, replica_groups=mesh['dz'=4,'dy'=2,'hi'=2,'lo'=2] {'dz','dy'}, dimensions={0}, use_global_device_ids=true | all-gather | bytes 18432 | tf_op jit(solution)/shard_map/all_gather | solution.py:607
  463.6 5.8 psum.87
  469.3 0.7 fusion.30
  470.4 1.0 fusion.10
  471.4 1.0 fusion.4
  472.4 31.3 %psum.88 = f32[16,256]{1,0:T(8,128)S(1)} all-reduce(f32[16,256]{1,0:T(8,128)S(1)} %fusion.10), channel_id=1, replica_groups=mesh['dz'=4,'dy'=2,'hi'=2,'lo'=2] {'dz','dy'}, use_global_device_ids=true, to_apply=%region_10.11 | all-reduce | flops 4096 | bytes 32768 | tf_op jit(solution)/shard_map/psum | solution.py:615
  503.8 1.1 fusion.15
  504.9 0.8 concatenate.58
  505.7 10.1 %psum.89 = f32[3360]{0:T(1024)S(1)} all-reduce(f32[3360]{0:T(1024)S(1)} %concatenate.58), channel_id=1, replica_groups=mesh['dz'=4,'dy'=2,'hi'=2,'lo'=2] {'hi','lo'}, use_global_device_ids=true, to_apply=%region_13.14 | all-reduce | flops 3360 | bytes 26880 | tf_op jit(solution)/shard_map/psum | solution.py:1456
  516.0 0.9 fusion.73
  516.9 1.3 fusion.71
  518.2 1.3 fusion.69
  519.5 0.8 fusion.76
  520.3 0.8 fusion.75
  521.2 1.3 fusion.67
  522.5 2.7 concatenate.59
  525.2 1.0 reshape.315
  526.4 34.4 %all-reduce.5 = (f32[2436]{0:T(1024)S(1)}, f32[6,2,128]{2,1,0:T(2,128)S(1)}) all-reduce(f32[2436]{0:T(1024)S(1)} %concatenate.59, f32[6,2,128]{2,1,0:T(2,128)S(1)} %copy.81), channel_id=1, replica_groups=mesh['dz'=4,'dy'=2,'hi'=2,'lo'=2] {'dz','dy'}, use_global_device_ids=true, to_apply=%region_26.27 | all-reduce | flops 3972 | bytes 31776 | tf_op jit(solution)/shard_map/psum | solution.py:1463
  567.6 0.7 multiply_reduce_fusion.8
  569.2 0.8 multiply_reduce_fusion.4
  571.5 2.6 concatenate.61
  574.3 0.8 copy.76
  575.1 44.0 %all-reduce.4 = (f32[]{:T(128)}, f32[10]{0:T(128)}, f32[10]{0:T(128)}, f32[6,2]{1,0:T(8,128)}, f32[6,2]{1,0:T(8,128)}) all-reduce(f32[]{:T(128)S(6)} %div.253, f32[10]{0:T(128)} %concatenate.61, f32[10]{0:T(128)} %concatenate.60, f32[6,2]{1,0:T(8,128)S(1)} %copy-done.29, ...), channel_id=1, replica_groups=mesh['dz'=4,'dy'=2,'hi'=2,'lo'=2] {'dz','dy','hi','lo'}, use_global_device_ids=true, to_apply=%region_4.5 | all-reduce | flops 45 | bytes 360 | tf_op jit(solution)/shard_map/psum | solution.py:1486
  619.1 1.4 fusion.79
  620.5 1.4 fusion.78
  621.9 1.3 maximum_divide_fusion.1
  623.3 1.2 maximum_divide_fusion.3
  625.9 1.8 multiply_subtract_fusion.2
  629.0 1.5 multiply_subtract_fusion.5
  631.8 1.7 multiply_subtract_fusion.4
  633.5 1.1 multiply_subtract_fusion.3
  634.7 0.8 copy.77
  635.5 1.7 multiply_subtract_fusion.1
  637.3 1.2 multiply_subtract_fusion
  (178 shorter events, 18.8 us)
Async XLA Ops:
  7.2 96.8 %copy-start.2 = (f32[2,128,256]{2,1,0:T(8,128)S(1)}, f32[2,128,256]{2,1,0:T(8,128)}, u32[]{:S(2)}) copy-start(f32[2,128,256]{2,1,0:T(8,128)} %param.32) | copy-start | bytes 786436
  7.2 93.8 %copy-start.9 = (f32[2,32,32,128]{3,2,1,0:T(8,128)S(1)}, f32[2,32,32,128]{3,2,1,0:T(8,128)}, u32[]{:S(2)}) copy-start(f32[2,32,32,128]{3,2,1,0:T(8,128)} %param.26) | copy-start | bytes 3145732
  7.2 96.4 %copy-start.17 = (f32[6,2,128]{2,1,0:T(2,128)S(1)}, f32[6,2,128]{2,1,0:T(2,128)}, u32[]{:S(2)}) copy-start(f32[6,2,128]{2,1,0:T(2,128)} %param.36) | copy-start | bytes 18436
  7.2 96.9 %copy-start.3 = (f32[3,576,128]{2,1,0:T(8,128)S(1)}, f32[3,576,128]{2,1,0:T(8,128)}, u32[]{:S(2)}) copy-start(f32[3,576,128]{2,1,0:T(8,128)} %param.30) | copy-start | bytes 2654212
  7.2 518.0 %reduce-scatter.5.cloned.1.call-start = ((), (), s32[]{:S(2)}) async-start(), calls=%async_computation.1 | async-start | bytes 196608
  21.7 0.6 copy-start.27
  21.7 0.6 copy-start.28
  53.1 1.8 copy-start.16
  54.9 45.8 %copy-start.11 = (bf16[128,506]{1,0:T(8,128)(2,1)}, bf16[128,506]{1,0:T(8,128)(2,1)S(1)}, u32[]{:S(2)}) copy-start(bf16[128,506]{1,0:T(8,128)(2,1)S(1)} %get-tuple-element.235) | copy-start | bytes 388612
  60.9 43.5 %copy-start.15 = (f32[16,128]{1,0:T(8,128)}, f32[16,128]{1,0:T(8,128)S(1)}, u32[]{:S(2)}) copy-start(f32[16,128]{1,0:T(8,128)S(1)} %psum.85) | copy-start | bytes 24580
  97.1 7.3 %copy-start.5 = (f32[2,576,128]{2,1,0:T(8,128)S(1)}, f32[2,576,128]{2,1,0:T(8,128)}, u32[]{:S(2)}) copy-start(f32[2,576,128]{2,1,0:T(8,128)} %param.31) | copy-start | bytes 1769476
  97.1 16.3 %collective-permute-start.3 = (f32[2,256]{1,0:T(2,128)S(1)}, f32[2,256]{1,0:T(2,128)S(1)}, u32[]{:S(2)}, u32[]{:S(2)}) collective-permute-start(f32[2,256]{1,0:T(2,128)S(1)} %bitcast.96), channel_id=1, source_target_pairs={{0,2},{2,0},{1,3},{3,1},{4,6},{6,4},{5,7},{7,5},{8,10},{10,8},{9,1... | collective-permute-start | bytes 6152 | tf_op jit(solution)/shard_map/ppermute | solution.py:533
  100.7 3.9 copy-start.12
  100.7 14.1 %collective-permute-start = (bf16[1024,128]{1,0:T(8,128)(2,1)}, bf16[1024,128]{1,0:T(8,128)(2,1)}, u32[]{:S(2)}, u32[]{:S(2)}) collective-permute-start(bf16[1024,128]{1,0:T(8,128)(2,1)} %bitcast.1), channel_id=1, source_target_pairs={{0,2},{2,0},{1,3},{3,1},{4,6},{6,4},{5,7},{7,5},{8,10},{10,8},{9,1... | collective-permute-start | bytes 786440 | tf_op jit(solution)/shard_map/ppermute | solution.py:533
  101.9 5.3 copy-start.13
  101.9 5.9 copy-start.41
  101.9 14.9 %collective-permute-start.1 = (f32[1024,128]{1,0:T(8,128)}, f32[1024,128]{1,0:T(8,128)S(1)}, u32[]{:S(2)}, u32[]{:S(2)}) collective-permute-start(f32[1024,128]{1,0:T(8,128)} %bitcast.3), channel_id=1, source_target_pairs={{0,2},{2,0},{1,3},{3,1},{4,6},{6,4},{5,7},{7,5},{8,10},{10,8},{9,1... | collective-permute-start | bytes 1572872 | tf_op jit(solution)/shard_map/ppermute | solution.py:533
  103.6 10.6 %collective-permute-start.2 = (f32[6,2,128]{2,1,0:T(2,128)S(1)}, f32[6,2,128]{2,1,0:T(2,128)S(1)}, u32[]{:S(2)}, u32[]{:S(2)}) collective-permute-start(f32[6,2,128]{2,1,0:T(2,128)S(1)} %copy-done.17), channel_id=1, source_target_pairs={{0,2},{2,0},{1,3},{3,1},{4,6},{6,4},{5,7},{7,5},{8,10},{10,8},{9,1... | collective-permute-start | bytes 18440 | tf_op jit(solution)/shard_map/ppermute | solution.py:533
  104.2 10.7 %copy-start.10 = (bf16[1,32,32,128]{3,2,1,0:T(8,128)(2,1)S(1)}, bf16[1,32,32,128]{3,2,1,0:T(8,128)(2,1)}, u32[]{:S(2)}) copy-start(bf16[1,32,32,128]{3,2,1,0:T(8,128)(2,1)} %get-tuple-element.227) | copy-start | bytes 786436
  424.2 6.3 copy-start.7
  425.9 10.8 %collective-permute-start.4 = (bf16[2,256]{1,0:T(2,128)(2,1)}, bf16[2,256]{1,0:T(2,128)(2,1)}, u32[]{:S(2)}, u32[]{:S(2)}) collective-permute-start(bf16[2,256]{1,0:T(2,128)(2,1)} %get-tuple-element.247), channel_id=1, source_target_pairs={{0,2},{2,0},{1,3},{3,1},{4,6},{6,4},{5,7},{7,5},{8,10},{10,8},{9,1... | collective-permute-start | bytes 3080 | tf_op jit(solution)/shard_map/ppermute | solution.py:533
  428.3 207.2 %copy-start.1 = (f32[2,576,128]{2,1,0:T(8,128)}, f32[2,576,128]{2,1,0:T(8,128)S(1)}, u32[]{:S(2)}) copy-start(f32[2,576,128]{2,1,0:T(8,128)S(1)} %get-tuple-element.300) | copy-start | bytes 1769476
  430.6 206.7 %copy-start = (f32[3,576,128]{2,1,0:T(8,128)}, f32[3,576,128]{2,1,0:T(8,128)S(1)}, u32[]{:S(2)}) copy-start(f32[3,576,128]{2,1,0:T(8,128)S(1)} %get-tuple-element.296) | copy-start | bytes 2654212
  434.7 126.8 %copy-start.42 = (f32[506]{0:T(512)S(1)}, f32[506]{0:T(512)}, u32[]{:S(2)}) copy-start(f32[506]{0:T(512)} %param.48) | copy-start | bytes 6076
  434.7 127.4 %copy-start.46 = (f32[256]{0:T(256)S(1)}, f32[256]{0:T(256)}, u32[]{:S(2)}) copy-start(f32[256]{0:T(256)} %param.46) | copy-start | bytes 3076
  434.7 127.9 %copy-start.43 = (f32[512]{0:T(512)S(1)}, f32[512]{0:T(512)}, u32[]{:S(2)}) copy-start(f32[512]{0:T(512)} %param.44) | copy-start | bytes 6148
  434.7 128.5 %copy-start.47 = (f32[2,128]{1,0:T(2,128)S(1)}, f32[2,128]{1,0:T(2,128)}, u32[]{:S(2)}) copy-start(f32[2,128]{1,0:T(2,128)} %param.40) | copy-start | bytes 3076
  434.7 129.1 %copy-start.44 = (f32[3,128]{1,0:T(4,128)S(1)}, f32[3,128]{1,0:T(4,128)}, u32[]{:S(2)}) copy-start(f32[3,128]{1,0:T(4,128)} %param.38) | copy-start | bytes 4612
  434.7 129.7 %copy-start.34 = (f32[6,2,128]{2,1,0:T(2,128)S(1)}, f32[6,2,128]{2,1,0:T(2,128)}, u32[]{:S(2)}) copy-start(f32[6,2,128]{2,1,0:T(2,128)} %param.49) | copy-start | bytes 18436
  434.8 133.7 %copy-start.45 = (f32[2,256]{1,0:T(2,128)S(1)}, f32[2,256]{1,0:T(2,128)}, u32[]{:S(2)}) copy-start(f32[2,256]{1,0:T(2,128)} %param.42) | copy-start | bytes 6148
  470.4 155.5 %copy-start.6 = (f32[128,506]{1,0:T(8,128)}, f32[128,506]{1,0:T(8,128)S(1)}, u32[]{:S(2)}) copy-start(f32[128,506]{1,0:T(8,128)S(1)} %get-tuple-element.316) | copy-start | bytes 777220
  504.9 69.3 %copy-start.14 = (f32[32,256]{1,0:T(8,128)}, f32[32,256]{1,0:T(8,128)S(1)}, u32[]{:S(2)}) copy-start(f32[32,256]{1,0:T(8,128)S(1)} %get-tuple-element.312) | copy-start | bytes 98308
  516.9 57.2 %copy-start.37 = (f32[2,128]{1,0:T(2,128)}, f32[2,128]{1,0:T(2,128)S(1)}, u32[]{:S(2)}) copy-start(f32[2,128]{1,0:T(2,128)S(1)} %get-tuple-element.305) | copy-start | bytes 3076
  518.2 55.9 %copy-start.49 = (f32[64]{0:T(128)}, f32[64]{0:T(128)S(1)}, u32[]{:S(2)}) copy-start(f32[64]{0:T(128)S(1)} %get-tuple-element.309) | copy-start | bytes 772
  519.5 54.6 %copy-start.50 = (f32[32]{0:T(128)}, f32[32]{0:T(128)S(1)}, u32[]{:S(2)}) copy-start(f32[32]{0:T(128)S(1)} %get-tuple-element.313) | copy-start | bytes 388
  520.3 107.4 %copy-start.19 = (f32[3,576]{1,0:T(4,128)}, f32[3,576]{1,0:T(4,128)S(1)}, u32[]{:S(2)}) copy-start(f32[3,576]{1,0:T(4,128)S(1)} %get-tuple-element.297) | copy-start | bytes 20740
  521.2 53.0 %copy-start.23 = (f32[2,576]{1,0:T(2,128)}, f32[2,576]{1,0:T(2,128)S(1)}, u32[]{:S(2)}) copy-start(f32[2,576]{1,0:T(2,128)S(1)} %get-tuple-element.301) | copy-start | bytes 13828
  522.5 51.7 %copy-start.51 = (f32[128]{0:T(128)}, f32[128]{0:T(128)S(1)}, u32[]{:S(2)}) copy-start(f32[128]{0:T(128)S(1)} %get-tuple-element.317) | copy-start | bytes 1540
  560.8 13.4 %copy-start.20 = (f32[6,2,128]{2,1,0:T(2,128)}, f32[6,2,128]{2,1,0:T(2,128)S(1)}, u32[]{:S(2)}) copy-start(f32[6,2,128]{2,1,0:T(2,128)S(1)} %get-tuple-element.320) | copy-start | bytes 18436
  562.1 12.1 %copy-start.24 = (f32[506]{0:T(512)}, f32[506]{0:T(512)S(1)}, u32[]{:S(2)}) copy-start(f32[506]{0:T(512)S(1)} %get-tuple-element.195) | copy-start | bytes 6076
  562.7 11.5 %copy-start.33 = (f32[256]{0:T(256)}, f32[256]{0:T(256)S(1)}, u32[]{:S(2)}) copy-start(f32[256]{0:T(256)S(1)} %get-tuple-element.197) | copy-start | bytes 3076
  563.8 10.4 %copy-start.31 = (f32[2,128]{1,0:T(2,128)}, f32[2,128]{1,0:T(2,128)S(1)}, u32[]{:S(2)}) copy-start(f32[2,128]{1,0:T(2,128)S(1)} %get-tuple-element.203) | copy-start | bytes 3076
  564.4 9.8 %copy-start.25 = (f32[3,128]{1,0:T(4,128)}, f32[3,128]{1,0:T(4,128)S(1)}, u32[]{:S(2)}) copy-start(f32[3,128]{1,0:T(4,128)S(1)} %get-tuple-element.205) | copy-start | bytes 4612
  566.3 7.9 %copy-start.40 = (f32[128]{0:T(128)}, f32[128]{0:T(128)S(1)}, u32[]{:S(2)}) copy-start(f32[128]{0:T(128)S(1)} %divide_rsqrt_fusion.3) | copy-start | bytes 1540
  567.0 7.3 %copy-start.39 = (f32[32]{0:T(128)}, f32[32]{0:T(128)S(1)}, u32[]{:S(2)}) copy-start(f32[32]{0:T(128)S(1)} %divide_rsqrt_fusion.4) | copy-start | bytes 388
  567.6 6.6 %copy-start.38 = (f32[64]{0:T(128)}, f32[64]{0:T(128)S(1)}, u32[]{:S(2)}) copy-start(f32[64]{0:T(128)S(1)} %divide_rsqrt_fusion.5) | copy-start | bytes 772
  568.3 6.8 %copy-start.29 = (f32[6,2]{1,0:T(8,128)S(1)}, f32[6,2]{1,0:T(8,128)}, u32[]{:S(2)}) copy-start(f32[6,2]{1,0:T(8,128)} %broadcast_multiply_fusion) | copy-start | bytes 148
  568.4 5.8 copy-start.30
  575.1 62.1 %copy-start.4 = (f32[3,576,128]{2,1,0:T(8,128)S(1)}, f32[3,576,128]{2,1,0:T(8,128)}, u32[]{:S(2)}) copy-start(f32[3,576,128]{2,1,0:T(8,128)} %param.30) | copy-start | bytes 2654212
  575.1 62.1 %copy-start.26 = (f32[3,128]{1,0:T(4,128)S(1)}, f32[3,128]{1,0:T(4,128)}, u32[]{:S(2)}) copy-start(f32[3,128]{1,0:T(4,128)} %copy-done.25) | copy-start | bytes 4612
  619.1 16.4 %copy-start.32 = (f32[2,128]{1,0:T(2,128)S(1)}, f32[2,128]{1,0:T(2,128)}, u32[]{:S(2)}) copy-start(f32[2,128]{1,0:T(2,128)} %copy-done.31) | copy-start | bytes 3076
  627.7 9.6 %copy-start.48 = (f32[3]{0:T(128)S(1)}, f32[3]{0:T(128)}, u32[]{:S(2)}) copy-start(f32[3]{0:T(128)} %maximum_divide_fusion.3) | copy-start | bytes 40
  634.6 3.8 copy-start.35
  634.6 3.8 copy-start.36
  635.5 3.0 copy-start.18
  635.5 3.0 copy-start.21
  635.5 3.0 copy-start.22
  635.5 3.7 copy-start.8
Sparse Core Ops, SparseCore 0:
  434.9 12.3 reduce-scatter.4
